TPU v7x, 32 devices: a whole 2x2x4 slice. The times are simulated.
32 devices in a mesh: slab: 8 (over y, x, core), probe: 4 (over z).
Axes of the slice: x: 2, y: 2, z: 4, core: 2. Of those that a mesh axis runs over, the one named last changes fastest.
Arguments:
- probes: float32 [8, 3, 16, 128, 128], P('probe', None, 'slab'), may hold values from -50 to 50
- earlier: float32 [16, 3, 16, 128, 128], P(None, None, 'slab', 'probe'), may hold values from -16 to 16
- modulus: float32 [16, 128, 128], P('slab'), may hold values from 0.5 to 2
- tangent: float32 [6, 16, 128, 128], P(None, 'slab'), may hold values from -0.3 to 2, as said below
Outputs:
- basis: float32 [8, 3, 16, 128, 128], P('probe', None, 'slab')
- correlation: float32 [16, 8], replicated
Inputs may be any that keep to these rules, and one draw needn't show every extreme that they name: `tangent`: entries 0 to 2 lie in 1 to 2, entries 3 to 5 in -0.3 to 0.3.
All inputs are finite; a program needn't handle non-finite values.
Results may differ from a plain program's by a relative error of at most 0.00014.
Values sent between devices are 32-bit elements; how exact they have to be, the bound alone decides.
A program may use at most 64 MiB of HBM per device.

v0:
```python
import jax
import jax.numpy as jnp
from jax import lax
from jax.sharding import PartitionSpec as P


def padded_2(cells, sides, width):
    for axis, dim in sides:
        count = lax.axis_size(axis)
        ends = count - 1
        head = lax.slice_in_dim(cells, 0, width, axis=dim)
        tail = lax.slice_in_dim(cells, cells.shape[dim] - width, cells.shape[dim], axis=dim)
        cells = jnp.concatenate(
            [
                lax.ppermute(tail, axis, [(i, (i + 1) % count) for i in range(ends)]),
                cells,
                lax.ppermute(head, axis, [((i + 1) % count, i) for i in range(ends)]),
            ],
            axis=dim,
        )
    return cells


def scaled_tangent(vectors, modulus, tensor):
    planes = vectors.shape[2] - 2
    height = vectors.shape[3]
    breadth = vectors.shape[4]
    padded = jnp.pad(vectors, ((0, 0), (0, 0), (0, 0), (1, 1), (1, 1)))
    mod_pad = jnp.pad(modulus, ((0, 0), (1, 1), (1, 1)))
    centre = padded[:, :, 1 : planes + 1, 1 : height + 1, 1 : breadth + 1]
    mod_centre = mod_pad[1 : planes + 1, 1 : height + 1, 1 : breadth + 1]
    summed = jnp.zeros_like(centre)
    for step_z in (-1, 0, 1):
        for step_y in (-1, 0, 1):
            for step_x in (-1, 0, 1):
                reach = abs(step_z) + abs(step_y) + abs(step_x)
                if reach == 0:
                    continue
                weight = (0.3, 0.1, 0.05)[reach - 1]
                nearby = padded[
                    :,
                    :,
                    1 + step_z : planes + 1 + step_z,
                    1 + step_y : height + 1 + step_y,
                    1 + step_x : breadth + 1 + step_x,
                ]
                mod_near = mod_pad[
                    1 + step_z : planes + 1 + step_z,
                    1 + step_y : height + 1 + step_y,
                    1 + step_x : breadth + 1 + step_x,
                ]
                edge_coef = 0.5 * weight * (mod_centre + mod_near)
                summed = summed + edge_coef * (centre - nearby)
    first_c = centre[:, 0]
    second_c = centre[:, 1]
    third_c = centre[:, 2]
    local_part = jnp.stack(
        [
            tensor[0] * first_c + tensor[3] * second_c + tensor[4] * third_c,
            tensor[3] * first_c + tensor[1] * second_c + tensor[5] * third_c,
            tensor[4] * first_c + tensor[5] * second_c + tensor[2] * third_c,
        ],
        axis=1,
    )
    return (summed + local_part - 8.0 * centre) / 8.0


def body(probes, earlier, modulus, tangent):
    depth = probes.shape[2]
    slabs = lax.axis_size("slab")
    highest = lax.Precision.HIGHEST
    ext_probe, ext_mod = (
        padded_2(probes, (("slab", 2),), 1),
        padded_2(modulus[None, None], (("slab", 2),), 1),
    )
    mod_wide = ext_mod[0, 0]
    first = scaled_tangent(ext_probe, mod_wide, tangent)
    ext_first = padded_2(first, (("slab", 2),), 1)
    second = scaled_tangent(ext_first, mod_wide, tangent)
    filtered = 2.0 * second - probes
    rows_y = lax.all_to_all(filtered, "probe", split_axis=3, concat_axis=0, tiled=True)
    flat_y = rows_y.reshape(rows_y.shape[0], -1)
    flat_q = earlier.reshape(earlier.shape[0], -1)
    scale = jnp.sqrt(jnp.float32(3 * depth * slabs * probes.shape[3] * probes.shape[4]))
    qq_part = jnp.dot(flat_q, flat_q.T, precision=highest)
    qy_part = jnp.dot(flat_q, flat_y.T, precision=highest)
    yy_part = jnp.dot(flat_y, flat_y.T, precision=highest)
    gram_earlier, cross, gram_filtered = lax.psum((qq_part, qy_part, yy_part), ("slab", "probe"))
    coeff = jax.scipy.linalg.cho_solve((jnp.linalg.cholesky(gram_earlier), True), cross)
    residue = flat_y - jnp.dot(coeff.T, flat_q, precision=highest)
    gram = gram_filtered - jnp.dot(cross.T, coeff, precision=highest)
    lower = jnp.linalg.cholesky(gram)
    basis_rows = jax.scipy.linalg.solve_triangular(lower, residue, lower=True)
    basis_rows = (basis_rows * scale).reshape(rows_y.shape)
    basis = lax.all_to_all(basis_rows, "probe", split_axis=0, concat_axis=3, tiled=True)
    return (basis, coeff * scale)


def solution(mesh):
    in_specs = (
        P("probe", None, "slab", None, None),
        P(None, None, "slab", "probe", None),
        P("slab", None, None),
        P(None, "slab", None, None),
    )
    out_specs = (P("probe", None, "slab", None, None), P())
    return jax.shard_map(body, mesh=mesh, in_specs=in_specs, out_specs=out_specs, check_vma=False)
```

profile of v0, /device:TPU:0, one launch (start us, length us, event | category | flops | bytes accessed | tf_op | source)
XLA Modules:
  0.0 160.9 jit_solution(15633891709158369731)
XLA Ops:
  0.6 0.0 copy-start
  0.7 1.0 fusion.194
  1.6 2.4 %collective-permute-start = (f32[1,1,1,128,128]{4,3,2,1,0:T(8,128)S(1)}, f32[1,1,1,128,128]{4,3,2,1,0:T(8,128)S(1)}, u32[]{:S(2)}, u32[]{:S(2)}) collective-permute-start(f32[1,1,1,128,128]{4,3,2,1,0:T(8,128)S(1)} %get-tuple-element.51), channel_id=1, source_target_pairs={{0,4},{4,8},{8,12},{12,16},{16,20},{20,24},{24,28},{1,5},{5,9},{9,... | collective-permute-start | bytes 196616 | tf_op jit(solution)/shard_map/ppermute | solution.py:15
  4.0 1.3 collective-permute-start.1
  5.3 1.2 fusion.193
  6.5 5.2 %collective-permute-start.2 = (f32[2,3,1,128,128]{4,3,2,1,0:T(8,128)S(1)}, f32[2,3,1,128,128]{4,3,2,1,0:T(8,128)S(1)}, u32[]{:S(2)}, u32[]{:S(2)}) collective-permute-start(f32[2,3,1,128,128]{4,3,2,1,0:T(8,128)S(1)} %get-tuple-element.15), channel_id=1, source_target_pairs={{0,4},{4,8},{8,12},{12,16},{16,20},{20,24},{24,28},{1,5},{5,9},{9,... | collective-permute-start | bytes 1179656 | tf_op jit(solution)/shard_map/ppermute | solution.py:15
  11.6 1.3 collective-permute-start.3
  12.9 1.3 slice_bitcast_fusion.5
  14.3 1.1 multiply_add_fusion.5
  15.4 0.2 fusion.131
  15.7 1.2 fusion.129
  17.0 1.5 select_maximum_fusion.2
  18.5 5.1 %broadcast_multiply_fusion = (f32[2,3,2,128,128]{4,3,2,1,0:T(8,128)S(1)}, f32[2,3,2,128,128]{4,3,2,1,0:T(8,128)S(1)}) fusion(f32[2,3,2,128,128]{4,3,2,1,0:T(8,128)S(1)} %copy-done, f32[2,1,2,128,128]{4,3,2,1,0:T(8,128)} %get-tuple-element.11, f32[2,1,2,128,128]{4,3,2,1,0:T(8,128)} %get-tuple-element.12, f32[2,1,2,128,128]{4,3,2,1,0:T(8,128)} %get-tuple-element.10, ...), kind=kLoop, calls=%fused_computation.212 | loop fusion | flops 16711680 | bytes 26214400 | tf_op jit(solution)/shard_map/div | solution.py:65
  23.8 0.1 fusion.192
  23.9 9.7 %collective-permute-start.4 = (f32[2,3,1,128,128]{4,3,2,1,0:T(8,128)S(1)}, f32[2,3,1,128,128]{4,3,2,1,0:T(8,128)S(1)}, u32[]{:S(2)}, u32[]{:S(2)}) collective-permute-start(f32[2,3,1,128,128]{4,3,2,1,0:T(8,128)S(1)} %get-tuple-element.13), channel_id=1, source_target_pairs={{0,4},{4,8},{8,12},{12,16},{16,20},{20,24},{24,28},{1,5},{5,9},{9,... | collective-permute-start | bytes 1179656 | tf_op jit(solution)/shard_map/ppermute | solution.py:15
  33.6 1.4 collective-permute-start.5
  35.0 2.2 %multiply_add_fusion.2 = (f32[2,1,2,128,128]{4,3,2,1,0:T(8,128)}, f32[2,1,2,128,128]{4,3,2,1,0:T(8,128)}, f32[2,1,2,128,128]{4,3,2,1,0:T(8,128)}) fusion(f32[2,3,2,128,128]{4,3,2,1,0:T(8,128)S(1)} %get-tuple-element.5, f32[2,128,128]{2,1,0:T(8,128)} %copy-done.25, f32[2,128,128]{2,1,0:T(8,128)} %copy-done.26, f32[2,128,128]{2,1,0:T(8,128)} %copy-done.23, ...), kind=kLoop, calls=%fused_computation.216 | loop fusion | flops 983040 | bytes 2359296 | tf_op jit(solution)/shard_map/add | solution.py:59
  37.2 0.1 collective-permute-done.5
  37.4 1.5 select_maximum_fusion
  38.8 5.6 %fusion.21 = f32[2,3,2,128,128]{4,3,2,1,0:T(8,128)S(1)} fusion(f32[2,3,2,128,128]{4,3,2,1,0:T(8,128)S(1)} %copy-done, f32[2,3,2,128,128]{4,3,2,1,0:T(8,128)S(1)} %get-tuple-element.6, f32[2,3,2,128,128]{4,3,2,1,0:T(8,128)S(1)} %get-tuple-element.5, f32[2,3,4,130,130]{4,3,2,1,0:T(8,128)S(1)} %select_maximum_fusion, ...), kind=kLoop, calls=%fused_computation.53 | loop fusion | flops 16711680 | bytes 27000832 | tf_op jit(solution)/shard_map/sub | solution.py:80
  44.5 1.5 copy.104
  46.0 4.9 %all-to-all-start = ((f32[2,3,2,128,128]{4,1,2,0,3:T(4,128)}), f32[2,3,2,128,128]{4,1,2,0,3:T(4,128)S(1)}, u32[]{:S(2)}, u32[]{:S(2)}) async-start(f32[2,3,2,128,128]{4,1,2,0,3:T(4,128)} %copy.104), calls=%async_computation | async-start | bytes 2097152 | tf_op jit(solution)/shard_map/all_to_all | solution.py:81
  50.8 2.7 %fusion.10 = f32[16,16]{0,1:T(8,128)S(1)} fusion(f32[16,3,2,32,128]{4,3,2,1,0:T(8,128)S(1)} %copy-done.1), kind=kOutput, calls=%fused_computation.44 | convolution fusion | flops 75497472 | bytes 1573888 | tf_op jit(solution)/shard_map/dot_general | solution.py:85
  53.6 21.8 %all-to-all-done = f32[2,3,2,128,128]{4,1,2,0,3:T(4,128)S(1)} async-done(((f32[2,3,2,128,128]{4,1,2,0,3:T(4,128)}), f32[2,3,2,128,128]{4,1,2,0,3:T(4,128)S(1)}, u32[]{:S(2)}, u32[]{:S(2)}) %all-to-all-start) | async-done | bytes 786464 | tf_op jit(solution)/shard_map/all_to_all | solution.py:81
  75.4 1.1 copy.136
  76.5 1.3 reshape.66
  77.8 1.8 %fusion.195 = f32[8,8]{0,1:T(8,128)S(1)} fusion(f32[8,24576]{1,0:T(8,128)S(1)} %reshape.66), kind=kOutput, calls=%fused_computation.307 | convolution fusion | flops 18874368 | bytes 786688 | tf_op jit(solution)/shard_map/dot_general | solution.py:87
  79.5 2.4 %fusion.13 = f32[16,8]{0,1:T(8,128)S(1)} fusion(f32[8,24576]{1,0:T(8,128)S(1)} %reshape.66, f32[2,8,192,128]{3,2,1,0:T(8,128)S(1)} %bitcast.83), kind=kOutput, calls=%fused_computation.46 | convolution fusion | flops 37748736 | bytes 2359808 | tf_op jit(solution)/shard_map/dot_general | solution.py:86
  82.0 44.0 %all-reduce.3 = (f32[16,8]{0,1:T(8,128)S(1)}, f32[16,16]{0,1:T(8,128)S(1)}, f32[8,8]{0,1:T(8,128)S(1)}) all-reduce(f32[16,8]{0,1:T(8,128)S(1)} %fusion.13, f32[16,16]{0,1:T(8,128)S(1)} %fusion.10, f32[8,8]{0,1:T(8,128)S(1)} %fusion.195), channel_id=1, replica_groups=mesh['slab'=8,'probe'=4] {'slab','probe'}, use_global_device_ids=true, to_apply=%region_1.2 | all-reduce | flops 448 | bytes 3584 | tf_op jit(solution)/shard_map/psum | solution.py:88
  126.0 0.1 copy.110
  126.1 1.5 cholesky.32
  127.6 0.6 compare_reduce_fusion.1
  128.2 0.6 fusion.182
  128.9 1.2 custom-call.17
  130.1 0.1 fusion.185
  130.2 0.7 broadcast_multiply_fusion.1
  131.0 1.7 %convolution_subtract_fusion = f32[8,24576]{1,0:T(8,128)S(1)} fusion(f32[8,24576]{1,0:T(8,128)S(1)} %reshape.66, f32[16,8]{0,1:T(8,128)S(1)} %get-tuple-element.54, f32[2,8,192,128]{3,2,1,0:T(8,128)S(1)} %bitcast.84), kind=kOutput, calls=%fused_computation.1 | convolution fusion | flops 37945344 | bytes 3146240 | tf_op jit(solution)/shard_map/dot_general | solution.py:90
  132.7 0.1 convolution_subtract_fusion.1
  132.8 0.1 copy.112
  132.9 0.7 cholesky.61
  133.6 0.1 select_reduce_fusion.1
  133.7 0.6 compare_reduce_fusion
  134.3 0.6 fusion.188
  135.0 0.6 custom-call.18
  135.6 0.8 convolution_multiply_fusion
  136.4 0.2 copy.114
  136.6 23.3 %all_to_all.33 = f32[8,3,2,32,128]{4,3,2,1,0:T(8,128)S(1)} all-to-all(f32[8,3,2,32,128]{4,3,2,1,0:T(8,128)S(1)} %copy.114), channel_id=1, replica_groups=mesh['slab'=8,'probe'=4] {'probe'}, dimensions={0} | all-to-all | bytes 1572864 | tf_op jit(solution)/shard_map/all_to_all | solution.py:95
  159.9 0.9 copy.115
  (66 shorter events, 0.2 us)
Async XLA Ops:
  0.6 14.7 %copy-start.2 = (f32[2,128,128]{2,1,0:T(8,128)S(1)}, f32[2,128,128]{2,1,0:T(8,128)}, u32[]{:S(2)}) copy-start(f32[2,128,128]{2,1,0:T(8,128)} %param.6) | copy-start | bytes 393220
  0.6 13.6 %copy-start = (f32[2,3,2,128,128]{4,3,2,1,0:T(8,128)S(1)}, f32[2,3,2,128,128]{4,3,2,1,0:T(8,128)}, u32[]{:S(2)}) copy-start(f32[2,3,2,128,128]{4,3,2,1,0:T(8,128)} %param.4) | copy-start | bytes 2359300
  1.6 13.7 %collective-permute-start = (f32[1,1,1,128,128]{4,3,2,1,0:T(8,128)S(1)}, f32[1,1,1,128,128]{4,3,2,1,0:T(8,128)S(1)}, u32[]{:S(2)}, u32[]{:S(2)}) collective-permute-start(f32[1,1,1,128,128]{4,3,2,1,0:T(8,128)S(1)} %get-tuple-element.51), channel_id=1, source_target_pairs={{0,4},{4,8},{8,12},{12,16},{16,20},{20,24},{24,28},{1,5},{5,9},{9,... | collective-permute-start | bytes 196616 | tf_op jit(solution)/shard_map/ppermute | solution.py:15
  4.0 11.4 %collective-permute-start.1 = (f32[1,1,1,128,128]{4,3,2,1,0:T(8,128)S(1)}, f32[1,1,1,128,128]{4,3,2,1,0:T(8,128)S(1)}, u32[]{:S(2)}, u32[]{:S(2)}) collective-permute-start(f32[1,1,1,128,128]{4,3,2,1,0:T(8,128)S(1)} %get-tuple-element.52), channel_id=1, source_target_pairs={{4,0},{8,4},{12,8},{16,12},{20,16},{24,20},{28,24},{5,1},{9,5},{13... | collective-permute-start | bytes 196616 | tf_op jit(solution)/shard_map/ppermute | solution.py:17
  6.5 10.5 %collective-permute-start.2 = (f32[2,3,1,128,128]{4,3,2,1,0:T(8,128)S(1)}, f32[2,3,1,128,128]{4,3,2,1,0:T(8,128)S(1)}, u32[]{:S(2)}, u32[]{:S(2)}) collective-permute-start(f32[2,3,1,128,128]{4,3,2,1,0:T(8,128)S(1)} %get-tuple-element.15), channel_id=1, source_target_pairs={{0,4},{4,8},{8,12},{12,16},{16,20},{20,24},{24,28},{1,5},{5,9},{9,... | collective-permute-start | bytes 1179656 | tf_op jit(solution)/shard_map/ppermute | solution.py:15
  11.6 5.4 %collective-permute-start.3 = (f32[2,3,1,128,128]{4,3,2,1,0:T(8,128)S(1)}, f32[2,3,1,128,128]{4,3,2,1,0:T(8,128)S(1)}, u32[]{:S(2)}, u32[]{:S(2)}) collective-permute-start(f32[2,3,1,128,128]{4,3,2,1,0:T(8,128)S(1)} %get-tuple-element.16), channel_id=1, source_target_pairs={{4,0},{8,4},{12,8},{16,12},{20,16},{24,20},{28,24},{5,1},{9,5},{13... | collective-permute-start | bytes 1179656 | tf_op jit(solution)/shard_map/ppermute | solution.py:17
  14.2 1.2 copy-start.23
  14.2 1.2 copy-start.24
  14.2 1.2 copy-start.25
  14.2 1.2 copy-start.26
  14.2 1.2 copy-start.27
  14.2 1.2 copy-start.28
  15.7 2.8 %copy-start.3 = (f32[2,128,128]{2,1,0:T(8,128)}, f32[2,128,128]{2,1,0:T(8,128)S(1)}, u32[]{:S(2)}) copy-start(f32[2,128,128]{2,1,0:T(8,128)S(1)} %get-tuple-element.49) | copy-start | bytes 393220
  15.7 8.0 %copy-start.5 = (f32[2,128,128]{2,1,0:T(8,128)}, f32[2,128,128]{2,1,0:T(8,128)S(1)}, u32[]{:S(2)}) copy-start(f32[2,128,128]{2,1,0:T(8,128)S(1)} %get-tuple-element.50) | copy-start | bytes 393220
  16.8 6.8 %copy-start.6 = (f32[2,128,128]{2,1,0:T(8,128)}, f32[2,128,128]{2,1,0:T(8,128)S(1)}, u32[]{:S(2)}) copy-start(f32[2,128,128]{2,1,0:T(8,128)S(1)} %get-tuple-element.23) | copy-start | bytes 393220
  16.8 6.8 %copy-start.7 = (f32[2,128,128]{2,1,0:T(8,128)}, f32[2,128,128]{2,1,0:T(8,128)S(1)}, u32[]{:S(2)}) copy-start(f32[2,128,128]{2,1,0:T(8,128)S(1)} %get-tuple-element.24) | copy-start | bytes 393220
  16.9 6.8 %copy-start.8 = (f32[2,128,128]{2,1,0:T(8,128)}, f32[2,128,128]{2,1,0:T(8,128)S(1)}, u32[]{:S(2)}) copy-start(f32[2,128,128]{2,1,0:T(8,128)S(1)} %get-tuple-element.25) | copy-start | bytes 393220
  16.9 6.8 %copy-start.9 = (f32[2,128,128]{2,1,0:T(8,128)}, f32[2,128,128]{2,1,0:T(8,128)S(1)}, u32[]{:S(2)}) copy-start(f32[2,128,128]{2,1,0:T(8,128)S(1)} %get-tuple-element.26) | copy-start | bytes 393220
  16.9 6.8 %copy-start.10 = (f32[2,128,128]{2,1,0:T(8,128)}, f32[2,128,128]{2,1,0:T(8,128)S(1)}, u32[]{:S(2)}) copy-start(f32[2,128,128]{2,1,0:T(8,128)S(1)} %get-tuple-element.27) | copy-start | bytes 393220
  16.9 6.8 %copy-start.11 = (f32[2,128,128]{2,1,0:T(8,128)}, f32[2,128,128]{2,1,0:T(8,128)S(1)}, u32[]{:S(2)}) copy-start(f32[2,128,128]{2,1,0:T(8,128)S(1)} %get-tuple-element.28) | copy-start | bytes 393220
  16.9 6.8 %copy-start.12 = (f32[2,128,128]{2,1,0:T(8,128)}, f32[2,128,128]{2,1,0:T(8,128)S(1)}, u32[]{:S(2)}) copy-start(f32[2,128,128]{2,1,0:T(8,128)S(1)} %get-tuple-element.29) | copy-start | bytes 393220
  16.9 6.8 %copy-start.13 = (f32[2,128,128]{2,1,0:T(8,128)}, f32[2,128,128]{2,1,0:T(8,128)S(1)}, u32[]{:S(2)}) copy-start(f32[2,128,128]{2,1,0:T(8,128)S(1)} %get-tuple-element.30) | copy-start | bytes 393220
  16.9 6.8 %copy-start.14 = (f32[2,128,128]{2,1,0:T(8,128)}, f32[2,128,128]{2,1,0:T(8,128)S(1)}, u32[]{:S(2)}) copy-start(f32[2,128,128]{2,1,0:T(8,128)S(1)} %get-tuple-element.31) | copy-start | bytes 393220
  16.9 6.8 %copy-start.15 = (f32[2,128,128]{2,1,0:T(8,128)}, f32[2,128,128]{2,1,0:T(8,128)S(1)}, u32[]{:S(2)}) copy-start(f32[2,128,128]{2,1,0:T(8,128)S(1)} %get-tuple-element.32) | copy-start | bytes 393220
  16.9 6.8 %copy-start.16 = (f32[2,128,128]{2,1,0:T(8,128)}, f32[2,128,128]{2,1,0:T(8,128)S(1)}, u32[]{:S(2)}) copy-start(f32[2,128,128]{2,1,0:T(8,128)S(1)} %get-tuple-element.33) | copy-start | bytes 393220
  16.9 6.8 %copy-start.17 = (f32[2,128,128]{2,1,0:T(8,128)}, f32[2,128,128]{2,1,0:T(8,128)S(1)}, u32[]{:S(2)}) copy-start(f32[2,128,128]{2,1,0:T(8,128)S(1)} %get-tuple-element.34) | copy-start | bytes 393220
  16.9 6.8 %copy-start.18 = (f32[2,128,128]{2,1,0:T(8,128)}, f32[2,128,128]{2,1,0:T(8,128)S(1)}, u32[]{:S(2)}) copy-start(f32[2,128,128]{2,1,0:T(8,128)S(1)} %get-tuple-element.35) | copy-start | bytes 393220
  16.9 6.8 %copy-start.19 = (f32[2,128,128]{2,1,0:T(8,128)}, f32[2,128,128]{2,1,0:T(8,128)S(1)}, u32[]{:S(2)}) copy-start(f32[2,128,128]{2,1,0:T(8,128)S(1)} %get-tuple-element.36) | copy-start | bytes 393220
  17.0 6.8 %copy-start.20 = (f32[2,128,128]{2,1,0:T(8,128)}, f32[2,128,128]{2,1,0:T(8,128)S(1)}, u32[]{:S(2)}) copy-start(f32[2,128,128]{2,1,0:T(8,128)S(1)} %get-tuple-element.37) | copy-start | bytes 393220
  17.0 6.8 %copy-start.21 = (f32[2,128,128]{2,1,0:T(8,128)}, f32[2,128,128]{2,1,0:T(8,128)S(1)}, u32[]{:S(2)}) copy-start(f32[2,128,128]{2,1,0:T(8,128)S(1)} %get-tuple-element.38) | copy-start | bytes 393220
  17.0 6.8 %copy-start.22 = (f32[2,128,128]{2,1,0:T(8,128)}, f32[2,128,128]{2,1,0:T(8,128)S(1)}, u32[]{:S(2)}) copy-start(f32[2,128,128]{2,1,0:T(8,128)S(1)} %get-tuple-element.39) | copy-start | bytes 393220
  23.9 13.4 %collective-permute-start.4 = (f32[2,3,1,128,128]{4,3,2,1,0:T(8,128)S(1)}, f32[2,3,1,128,128]{4,3,2,1,0:T(8,128)S(1)}, u32[]{:S(2)}, u32[]{:S(2)}) collective-permute-start(f32[2,3,1,128,128]{4,3,2,1,0:T(8,128)S(1)} %get-tuple-element.13), channel_id=1, source_target_pairs={{0,4},{4,8},{8,12},{12,16},{16,20},{20,24},{24,28},{1,5},{5,9},{9,... | collective-permute-start | bytes 1179656 | tf_op jit(solution)/shard_map/ppermute | solution.py:15
  33.6 5.2 %copy-start.4 = (f32[2,128,128]{2,1,0:T(8,128)S(1)}, f32[2,128,128]{2,1,0:T(8,128)}, u32[]{:S(2)}) copy-start(f32[2,128,128]{2,1,0:T(8,128)} %copy-done.3) | copy-start | bytes 393220
  33.6 3.7 %collective-permute-start.5 = (f32[2,3,1,128,128]{4,3,2,1,0:T(8,128)S(1)}, f32[2,3,1,128,128]{4,3,2,1,0:T(8,128)S(1)}, u32[]{:S(2)}, u32[]{:S(2)}) collective-permute-start(f32[2,3,1,128,128]{4,3,2,1,0:T(8,128)S(1)} %get-tuple-element.14), channel_id=1, source_target_pairs={{4,0},{8,4},{12,8},{16,12},{20,16},{24,20},{28,24},{5,1},{9,5},{13... | collective-permute-start | bytes 1179656 | tf_op jit(solution)/shard_map/ppermute | solution.py:17
  44.4 6.4 %copy-start.1 = (f32[16,3,2,32,128]{4,3,2,1,0:T(8,128)S(1)}, f32[16,3,2,32,128]{4,3,2,1,0:T(8,128)}, u32[]{:S(2)}) copy-start(f32[16,3,2,32,128]{4,3,2,1,0:T(8,128)} %param.5) | copy-start | bytes 4718596
  46.0 29.4 %all-to-all-start = ((f32[2,3,2,128,128]{4,1,2,0,3:T(4,128)}), f32[2,3,2,128,128]{4,1,2,0,3:T(4,128)S(1)}, u32[]{:S(2)}, u32[]{:S(2)}) async-start(f32[2,3,2,128,128]{4,1,2,0,3:T(4,128)} %copy.104), calls=%async_computation | async-start | bytes 2097152 | tf_op jit(solution)/shard_map/all_to_all | solution.py:81
where the time goes:
time: 161 us
  blocking collectives  67.4 us (42%)
  starting transfers between devices  26.1 us (16%)
  other arithmetic  25 us (16%)
  waiting for transfers between devices  21.9 us (14%)
  matrix products  10.5 us (7%)
  local copies, waits for them, and re-layouts  8.73 us (5%)
    psum x1, blocking collectives, body(): lax.psum((qq_part, qy_part, yy_part), ('slab', 'probe'))  44 us
    all_to_all x1, blocking collectives, body(): lax.all_to_all(basis_rows, 'probe', split_axis=0, concat_axis=3, tiled=True)  23.3 us
    all_to_all x1, waiting for transfers between devices, body(): lax.all_to_all(filtered, 'probe', split_axis=3, concat_axis=0, tiled=True)  21.8 us
    ppermute x3, starting transfers between devices, padded_2(): lax.ppermute(tail, axis, [(i, (i + 1) % count) for i in range(ends)])  17.2 us
    sub x1, other arithmetic, body(): filtered = 2.0 * second - probes  5.59 us
    div x1, other arithmetic, scaled_tangent(): return (summed + local_part - 8.0 * centre) / 8.0  5.13 us
    all_to_all x1, starting transfers between devices, body(): lax.all_to_all(filtered, 'probe', split_axis=3, concat_axis=0, tiled=True)  4.87 us
    ppermute x3, starting transfers between devices, padded_2(): lax.ppermute(head, axis, [((i + 1) % count, i) for i in range(ends)])  4.01 us
  transfers between devices with their start and end apart: 7, of which 2 were waited for; matrix products, arithmetic and copies ran while one was open for 6% of the time, Pallas kernels for 0%

commit v1 on v0

v1 whole, which is shorter than its diff:
```python
import functools

import jax
import jax.numpy as jnp
from jax import lax
from jax.experimental import pallas as pl
from jax.experimental.pallas import tpu as pltpu
from jax.sharding import PartitionSpec as P

MESH = pl.DeviceIdType.MESH
LANES = 128
PAD = 8
GROUP = 4


def neighbour_sum(ref, lead, z, start, rows):
    def at(plane, off):
        return ref[lead + (plane, pl.ds(PAD + start + off, rows), slice(None))]

    centre = at(z, 0)
    beside = at(z, -1) + at(z, 1)
    above = at(z - 1, 0) + at(z + 1, 0)
    corner = (at(z - 1, -1) + at(z + 1, -1)) + (at(z - 1, 1) + at(z + 1, 1))
    along = 0.3 * centre + 0.1 * (above + beside) + 0.05 * corner
    still = 0.3 * (above + beside) + 0.1 * corner
    width = along.shape[-1]
    lane = lax.broadcasted_iota(jnp.int32, along.shape, 1)
    from_left = jnp.where(lane == 0, 0.0, pltpu.roll(along, 1, 1))
    from_right = jnp.where(lane == width - 1, 0.0, pltpu.roll(along, width - 1, 1))
    return still + from_left + from_right


def spread(column, shape):
    return jnp.broadcast_to(column, shape)


def kernel(
    slabs, groups, scale,
    probes_ref, earlier_ref, modulus_ref, tangent_ref,
    basis_ref, corr_ref,
    v0, v1, g0, g1, mod, ten, diag, quick, filt, every, outgoing,
    acc_q, acc_y, slots_q, slots_qp, slots_y, slots_yp, inverse, mixing,
    load_sem, halo_send, halo_recv, mod_send, mod_recv,
    there_send, there_recv, back_send, back_recv,
    sum_send, sum_recv, sump_send, sump_recv, own_sem,
):
    slab = lax.axis_index("slab")
    group = lax.axis_index("probe")
    mine, _, depth, height, _ = probes_ref.shape
    known, fields, share, _ = earlier_ref.shape
    total = mine * groups
    rows = 32

    loads = [
        pltpu.make_async_copy(modulus_ref, mod.at[pl.ds(1, depth), pl.ds(PAD, height), :], load_sem.at[0]),
        pltpu.make_async_copy(tangent_ref, ten, load_sem.at[1]),
        pltpu.make_async_copy(earlier_ref, quick, load_sem.at[2]),
    ]
    for r in range(mine):
        loads.append(
            pltpu.make_async_copy(
                probes_ref.at[r],
                v0.at[r, :, pl.ds(1, depth), pl.ds(PAD, height), :],
                load_sem.at[3 + r],
            )
        )
    for copy in loads:
        copy.start()

    barrier = pltpu.get_barrier_semaphore()
    for o in range(1, slabs):
        pl.semaphore_signal(barrier, inc=1, device_id={"slab": lax.rem(slab + o, slabs)}, device_id_type=MESH)
    for o in range(1, groups):
        pl.semaphore_signal(barrier, inc=1, device_id={"probe": lax.rem(group + o, groups)}, device_id_type=MESH)

    for ref in (v0, v1):
        edge = jnp.zeros(ref.shape[:3] + (PAD, LANES), jnp.float32)
        ref[:, :, :, pl.ds(0, PAD), :] = edge
        ref[:, :, :, pl.ds(PAD + height, PAD), :] = edge
    edge = jnp.zeros((depth + 2, PAD, LANES), jnp.float32)
    mod[:, pl.ds(0, PAD), :] = edge
    mod[:, pl.ds(PAD + height, PAD), :] = edge

    def clear(plane):
        for ref in (v0, v1):
            ref[:, :, plane, pl.ds(PAD, height), :] = jnp.zeros((mine, 3, height, LANES), jnp.float32)
        mod[plane, pl.ds(PAD, height), :] = jnp.zeros((height, LANES), jnp.float32)

    @pl.when(slab == 0)
    def _():
        clear(0)

    @pl.when(slab == slabs - 1)
    def _():
        clear(depth + 1)

    pl.semaphore_wait(barrier, slabs + groups - 2)

    towards = (lax.rem(slab + slabs - 1, slabs), lax.rem(slab + 1, slabs))
    can_send = (slab > 0, slab < slabs - 1)
    can_recv = (slab < slabs - 1, slab > 0)
    lands = (depth + 1, 0)

    def mod_copy(way):
        return pltpu.make_async_remote_copy(
            src_ref=modulus_ref.at[(0, depth - 1)[way]],
            dst_ref=mod.at[lands[way], pl.ds(PAD, height), :],
            send_sem=mod_send.at[way],
            recv_sem=mod_recv.at[way],
            device_id={"slab": towards[way]},
            device_id_type=MESH,
        )

    def halo_copy(stage, r, way):
        if stage == 0:
            source, into = probes_ref.at[r, :, (0, depth - 1)[way]], v0
        else:
            source, into = v1.at[r, :, (1, depth)[way], pl.ds(PAD, height), :], v1
        return pltpu.make_async_remote_copy(
            src_ref=source,
            dst_ref=into.at[r, :, lands[way], pl.ds(PAD, height), :],
            send_sem=halo_send.at[stage, r, way],
            recv_sem=halo_recv.at[stage, r, way],
            device_id={"slab": towards[way]},
            device_id_type=MESH,
        )

    def guarded(condition, act):
        @pl.when(condition)
        def _():
            act()

    for way in range(2):
        def begin(way=way):
            mod_copy(way).start()
            for r in range(mine):
                halo_copy(0, r, way).start()
        guarded(can_send[way], begin)

    def products(first, second, acc_ref, rows_at, cols_at, mirror_at):
        def step(f, accs):
            left = [ref[k, f] for ref, k in first]
            right = [ref[k, f] for ref, k in second]
            out = []
            n = 0
            for a in left:
                for b in right:
                    prod = a * b
                    part = accs[n]
                    for t in range(share // 8):
                        part = part + prod[8 * t : 8 * t + 8]
                    out.append(part)
                    n += 1
            return tuple(out)

        zero = jnp.zeros((8, LANES), jnp.float32)
        accs = lax.fori_loop(0, fields, step, (zero,) * (len(first) * len(second)))
        n = 0
        for i in range(len(first)):
            for j in range(len(second)):
                acc_ref[cols_at[i], rows_at[j]] = accs[n]
                if mirror_at is not None:
                    col, row = mirror_at(i, j)
                    acc_ref[col, row] = accs[n]
                n += 1

    def collapse(acc_ref, cols, count):
        lane = lax.broadcasted_iota(jnp.int32, (count, LANES), 1)
        result = jnp.zeros((count, LANES), jnp.float32)
        for v in range(cols):
            summed = jnp.sum(jnp.sum(acc_ref[v], axis=1), axis=1, keepdims=True)
            result = jnp.where(lane == v, spread(summed, (count, LANES)), result)
        return result

    def share_copy(slots, axis, me, count, o, sends, recvs):
        return pltpu.make_async_remote_copy(
            src_ref=slots.at[me],
            dst_ref=slots.at[me],
            send_sem=sends.at[o],
            recv_sem=recvs.at[o],
            device_id={axis: lax.rem(me + o, count)},
            device_id_type=MESH,
        )

    def share_start(slots, axis, me, count, sends, recvs, value):
        slots[me] = value
        for o in range(1, count):
            share_copy(slots, axis, me, count, o, sends, recvs).start()

    def share_finish(slots, axis, me, count, sends, recvs):
        for o in range(1, count):
            share_copy(slots, axis, me, count, o, sends, recvs).wait()
        value = slots[0]
        for i in range(1, count):
            value = value + slots[i]
        return value

    loads[2].wait()
    for i in range(0, known, GROUP):
        for j in range(i, known, GROUP):
            left = list(range(i, i + GROUP))
            right = list(range(j, j + GROUP))
            products(
                [(quick, k) for k in left], [(quick, k) for k in right], acc_q, right, left,
                (lambda a, b, left=left, right=right: (right[b], left[a])) if i != j else None,
            )
    share_start(slots_q, "slab", slab, slabs, sum_send.at[0], sum_recv.at[0], collapse(acc_q, known, known))

    loads[0].wait()
    loads[1].wait()
    for way in range(2):
        guarded(can_recv[way], lambda way=way: mod_copy(way).wait_recv())

    def coefficients(z, carry):
        for start in range(0, height, rows):
            here = pl.ds(start, rows)
            m = mod[z + 1, pl.ds(PAD + start, rows), :]
            base = (3.4 * m + neighbour_sum(mod, (), z + 1, start, rows)) * 0.0625 - 1.0
            for c in range(3):
                diag[c, z, here, :] = base + 0.125 * ten[c, z, here, :]
        return carry

    lax.fori_loop(0, depth, coefficients, 0)

    def halo_products(stage, r, way):
        v, g = ((v0, g0), (v1, g1))[stage]
        plane = lands[way]
        for c in range(3):
            g[r, c, plane] = mod[plane] * v[r, c, plane]

    def apply(stage, r):
        v, g = ((v0, g0), (v1, g1))[stage]

        def body(z, carry):
            for start in range(0, height, rows):
                here = pl.ds(start, rows)
                inner = pl.ds(PAD + start, rows)
                m = mod[z + 1, inner, :]
                vec = [v[r, c, z + 1, inner, :] for c in range(3)]
                cross = [0.125 * ten[3 + c, z, here, :] for c in range(3)]
                mixed = (
                    cross[0] * vec[1] + cross[1] * vec[2],
                    cross[0] * vec[0] + cross[2] * vec[2],
                    cross[1] * vec[0] + cross[2] * vec[1],
                )
                for c in range(3):
                    out = diag[c, z, here, :] * vec[c] + mixed[c]
                    near = m * neighbour_sum(v, (r, c), z + 1, start, rows) + neighbour_sum(
                        g, (r, c), z + 1, start, rows
                    )
                    out = out - 0.0625 * near
                    if stage == 0:
                        v1[r, c, z + 1, inner, :] = out
                        g1[r, c, z + 1, inner, :] = m * out
                    else:
                        filt[r, c * depth + z, here, :] = 2.0 * out - v0[r, c, z + 1, inner, :]
            return carry

        lax.fori_loop(0, depth, body, 0)

    def wait_halo(stage, r):
        for way in range(2):
            guarded(can_recv[way], lambda way=way: halo_copy(stage, r, way).wait_recv())
            halo_products(stage, r, way)

    for r in range(mine):
        loads[3 + r].wait()
        for c in range(3):
            for z in range(1, depth + 1):
                g0[r, c, z] = mod[z] * v0[r, c, z]
                blank = jnp.zeros((PAD, LANES), jnp.float32)
                g1[r, c, z, pl.ds(0, PAD), :] = blank
                g1[r, c, z, pl.ds(PAD + height, PAD), :] = blank
        wait_halo(0, r)
        apply(0, r)
        for way in range(2):
            guarded(can_send[way], lambda way=way, r=r: halo_copy(1, r, way).start())

    partial = share_finish(slots_q, "slab", slab, slabs, sum_send.at[0], sum_recv.at[0])
    share_start(slots_qp, "probe", group, groups, sump_send.at[0], sump_recv.at[0], partial)

    order = sorted(range(1, groups), key=lambda o: (abs(o - groups // 2), o))

    def there_copy(r, o):
        to = lax.rem(group + o, groups)
        return pltpu.make_async_remote_copy(
            src_ref=filt.at[r, :, pl.ds(pl.multiple_of(to * share, share), share), :],
            dst_ref=every.at[group * mine + r],
            send_sem=there_send.at[r, o],
            recv_sem=there_recv.at[r, o],
            device_id={"probe": to},
            device_id_type=MESH,
        )

    own_rows = pl.ds(pl.multiple_of(group * share, share), share)
    for r in range(mine):
        wait_halo(1, r)
        apply(1, r)
        for o in order:
            there_copy(r, o).start()
        keep = pltpu.make_async_copy(filt.at[r, :, own_rows, :], every.at[group * mine + r], own_sem.at[r])
        keep.start()

    gram_q = share_finish(slots_qp, "probe", group, groups, sump_send.at[0], sump_recv.at[0])
    square = (known, LANES)
    lane = lax.broadcasted_iota(jnp.int32, square, 1)
    line = lax.broadcasted_iota(jnp.int32, square, 0)
    table = jnp.where(lane < known, gram_q, 0.0) + jnp.where(lane == line + known, 1.0, 0.0)
    for k in range(known):
        column = spread(table[:, k : k + 1], square)
        pivot = spread(column[k : k + 1, :], square)
        lead = spread(table[k : k + 1, :], square) / pivot
        table = jnp.where(line == k, lead, table - column * lead)
    inverse[...] = pltpu.roll(table, LANES - known, 1)
    inv = jnp.where(lane < known, inverse[...], 0.0)
    inverse[...] = inv

    def batch(r):
        ids = [p * mine + r for p in range(groups)]
        return [ids[i : i + GROUP] for i in range(0, groups, GROUP)]

    for r in range(mine):
        pltpu.make_async_copy(filt.at[r, :, own_rows, :], every.at[group * mine + r], own_sem.at[r]).wait()
        for o in order:
            there_copy(r, o).wait_recv()
        for ids in batch(r):
            for i in range(0, known, GROUP):
                left = list(range(i, i + GROUP))
                products([(quick, k) for k in left], [(every, k) for k in ids], acc_y, ids, left, None)
            for before in range(r + 1):
                for old in batch(before):
                    if before == r and old[0] > ids[0]:
                        continue
                    same = old == ids
                    products(
                        [(every, k) for k in old], [(every, k) for k in ids], acc_y, ids,
                        [known + k for k in old],
                        None if same else (lambda a, b, old=old, ids=ids: (known + ids[b], old[a])),
                    )
    part = collapse(acc_y, known + total, total)
    share_start(slots_y, "slab", slab, slabs, sum_send.at[1], sum_recv.at[1], part)
    part = share_finish(slots_y, "slab", slab, slabs, sum_send.at[1], sum_recv.at[1])
    share_start(slots_yp, "probe", group, groups, sump_send.at[1], sump_recv.at[1], part)
    gram_y = share_finish(slots_yp, "probe", group, groups, sump_send.at[1], sump_recv.at[1])

    flat = (total, LANES)
    lane = lax.broadcasted_iota(jnp.int32, flat, 1)
    line = lax.broadcasted_iota(jnp.int32, flat, 0)
    cross = jnp.where(lane < known, gram_y, 0.0)
    coeff = jnp.zeros(flat, jnp.float32)
    for k in range(known):
        coeff = coeff + spread(cross[:, k : k + 1], flat) * spread(inverse[k : k + 1, :], flat)
    nt = (((1,), (1,)), ((), ()))
    taken = lax.dot_general(
        coeff, jnp.concatenate([cross, jnp.zeros((LANES - total, LANES), jnp.float32)], axis=0), nt,
        precision=lax.Precision.HIGHEST, preferred_element_type=jnp.float32,
    )
    at = known + total
    gram = pltpu.roll(gram_y, LANES - known, 1) - taken
    gram = jnp.where(lane < total, gram, 0.0)
    work = pltpu.roll(gram, at, 1) + jnp.where(lane == line + known, 1.0, 0.0) - coeff
    factor = jnp.ones(flat, jnp.float32)
    for k in range(total):
        column = spread(work[:, at + k : at + k + 1], flat)
        pivot = spread(column[k : k + 1, :], flat)
        lead = spread(work[k : k + 1, :], flat) / pivot
        factor = jnp.where(line == k, pivot, factor)
        work = jnp.where(line > k, work - column * lead, work)
    mixing[...] = work * (scale / jnp.sqrt(factor))

    def make(i):
        weights = mixing[pl.ds(i, 1), :]
        splats = [spread(weights[:, v : v + 1], (8, LANES)) for v in range(known + total)]

        def step(f, carry):
            for t in range(share // 8):
                sub = pl.ds(8 * t, 8)
                value = splats[0] * quick[0, f, sub, :]
                for v in range(1, known):
                    value = value + splats[v] * quick[v, f, sub, :]
                for v in range(total):
                    value = value + splats[known + v] * every[v, f, sub, :]
                outgoing[i, f, sub, :] = value
            return carry

        lax.fori_loop(0, fields, step, 0)

    def back_copy(r, o):
        to = lax.rem(group + o, groups)
        return pltpu.make_async_remote_copy(
            src_ref=outgoing.at[to * mine + r],
            dst_ref=basis_ref.at[r, :, own_rows, :],
            send_sem=back_send.at[r, o],
            recv_sem=back_recv.at[r, o],
            device_id={"probe": to},
            device_id_type=MESH,
        )

    def own_copy(r):
        return pltpu.make_async_copy(
            outgoing.at[group * mine + r], basis_ref.at[r, :, own_rows, :], own_sem.at[mine + r]
        )

    for o in order:
        for r in range(mine):
            make(lax.rem(group + o, groups) * mine + r)
            back_copy(r, o).start()
    for r in range(mine):
        make(group * mine + r)
        own_copy(r).start()

    corr = lax.dot_general(
        inverse[...], cross, nt, precision=lax.Precision.HIGHEST, preferred_element_type=jnp.float32
    )
    corr_ref[...] = corr * scale

    for way in range(2):
        def finish(way=way):
            mod_copy(way).wait_send()
            for stage in range(2):
                for r in range(mine):
                    halo_copy(stage, r, way).wait_send()
        guarded(can_send[way], finish)
    for r in range(mine):
        own_copy(r).wait()
        for o in order:
            there_copy(r, o).wait_send()
            back_copy(r, o).wait()


def body(probes, earlier, modulus, tangent):
    mine, parts, depth, height, width = probes.shape
    known, _, _, share, _ = earlier.shape
    slabs = lax.axis_size("slab")
    groups = lax.axis_size("probe")
    total = mine * groups
    fields = parts * depth
    scale = float(parts * depth * slabs * height * width) ** 0.5
    f32 = jnp.float32
    padded = (mine, parts, depth + 2, height + 2 * PAD, width)
    dma = pltpu.SemaphoreType.DMA
    anywhere = pl.BlockSpec(memory_space=pl.ANY)
    basis, corr = pl.pallas_call(
        functools.partial(kernel, slabs, groups, scale),
        out_shape=(
            jax.ShapeDtypeStruct((mine, fields, height, width), f32),
            jax.ShapeDtypeStruct((known, total), f32),
        ),
        in_specs=[anywhere] * 4,
        out_specs=(anywhere, pl.BlockSpec(memory_space=pltpu.VMEM)),
        scratch_shapes=[
            pltpu.VMEM(padded, f32),
            pltpu.VMEM(padded, f32),
            pltpu.VMEM(padded, f32),
            pltpu.VMEM(padded, f32),
            pltpu.VMEM((depth + 2, height + 2 * PAD, width), f32),
            pltpu.VMEM((6, depth, height, width), f32),
            pltpu.VMEM((3, depth, height, width), f32),
            pltpu.VMEM((known, fields, share, width), f32),
            pltpu.VMEM((mine, fields, height, width), f32),
            pltpu.VMEM((total, fields, share, width), f32),
            pltpu.VMEM((total, fields, share, width), f32),
            pltpu.VMEM((known, known, 8, width), f32),
            pltpu.VMEM((known + total, total, 8, width), f32),
            pltpu.VMEM((slabs, known, LANES), f32),
            pltpu.VMEM((groups, known, LANES), f32),
            pltpu.VMEM((slabs, total, LANES), f32),
            pltpu.VMEM((groups, total, LANES), f32),
            pltpu.VMEM((known, LANES), f32),
            pltpu.VMEM((total, LANES), f32),
            dma((3 + mine,)),
            dma((2, mine, 2)),
            dma((2, mine, 2)),
            dma((2,)),
            dma((2,)),
            dma((mine, groups)),
            dma((mine, groups)),
            dma((mine, groups)),
            dma((mine, groups)),
            dma((2, slabs)),
            dma((2, slabs)),
            dma((2, groups)),
            dma((2, groups)),
            dma((2 * mine,)),
        ],
        compiler_params=pltpu.CompilerParams(
            collective_id=0, has_side_effects=True, vmem_limit_bytes=40 * 1024 * 1024
        ),
    )(probes, earlier.reshape(known, fields, share, width), modulus, tangent)
    return basis.reshape(probes.shape), corr


def solution(mesh):
    in_specs = (
        P("probe", None, "slab", None, None),
        P(None, None, "slab", "probe", None),
        P("slab", None, None),
        P(None, "slab", None, None),
    )
    out_specs = (P("probe", None, "slab", None, None), P())
    return jax.shard_map(body, mesh=mesh, in_specs=in_specs, out_specs=out_specs, check_vma=False)
```

time: 161 us -> 70.3 us (0.44)
  blocking collectives: 67.4 us -> 0 us
  Pallas kernels: 0 us -> 62.7 us
  starting transfers between devices: 26.1 us -> 0 us
  other arithmetic: 25 us -> 0 us
  waiting for transfers between devices: 21.9 us -> 0 us
  matrix products: 10.5 us -> 0 us
  local copies, waits for them, and re-layouts: 8.73 us -> 6.11 us
    pallas_call x0 -> x1, Pallas kernels: none -> 62.7 us  [body(): pl.pallas_call(functools.partial(kernel, slabs, groups, scale), out_shape...]
    psum x1 -> x0, blocking collectives: 44 us -> none  [body(): lax.psum((qq_part, qy_part, yy_part), ('slab', 'probe'))]
    all_to_all x1 -> x0, blocking collectives: 23.3 us -> none  [body(): lax.all_to_all(basis_rows, 'probe', split_axis=0, concat_axis=3, tiled=True)]
    all_to_all x1 -> x0, waiting for transfers between devices: 21.8 us -> none  [body(): lax.all_to_all(filtered, 'probe', split_axis=3, concat_axis=0, tiled=True)]
    ppermute x6 -> x0, starting transfers between devices: 21.2 us -> none  [the longest x3 17.2 us: padded_2(): lax.ppermute(tail, axis, [(i, (i + 1) % count) for i in range(ends)])]
    dot_general x5 -> x0, matrix products: 8.76 us -> none  [the longest x1 2.72 us: body(): qq_part = jnp.dot(flat_q, flat_q.T, precision=highest)]
    another operation x10 -> x0, other arithmetic: 6.68 us -> none  [the longest x3 2.13 us: body(): jnp.linalg.cholesky(gram_earlier)]
    unnamed x58 -> x10, local copies, waits for them, and re-layouts: 0.12 us -> 6.11 us
  transfers between devices with their start and end apart: 7 -> 0, of which waited for: 2 -> 0; matrix products, arithmetic and copies ran while one was open for 6% -> 0% of each run, Pallas kernels for 0% -> 0%
where the time goes in v1:
time: 70.3 us; the launch traced here: 69.5 us
  Pallas kernels  62.7 us (89%)
  local copies, waits for them, and re-layouts  6.11 us (9%)
    pallas_call x1, Pallas kernels, body(): pl.pallas_call(functools.partial(kernel, slabs, groups, scale), out_shape...  62.7 us
    unnamed x10, local copies, waits for them, and re-layouts  6.11 us

profile of v1, /device:TPU:0, one launch (start us, length us, event | category | flops | bytes accessed | tf_op | source)
XLA Modules:
  0.0 69.5 jit_solution(7444714358625626965)
XLA Ops:
  0.6 0.0 copy-start
  0.6 1.4 %copy-done = f32[16,3,2,32,128]{4,3,2,1,0:T(8,128)S(1)} copy-done((f32[16,3,2,32,128]{4,3,2,1,0:T(8,128)S(1)}, f32[16,3,2,32,128]{4,3,2,1,0:T(8,128)}, u32[]{:S(2)}) %copy-start) | copy-done | bytes 1572888
  2.0 0.0 copy-start.1
  2.0 1.1 %copy-done.1 = f32[2,3,2,128,128]{4,3,2,1,0:T(8,128)S(1)} copy-done((f32[2,3,2,128,128]{4,3,2,1,0:T(8,128)S(1)}, f32[2,3,2,128,128]{4,3,2,1,0:T(8,128)}, u32[]{:S(2)}) %copy-start.1) | copy-done | bytes 786456
  3.2 0.0 copy-start.2
  3.2 1.1 %copy-done.2 = f32[6,2,128,128]{3,2,1,0:T(8,128)S(1)} copy-done((f32[6,2,128,128]{3,2,1,0:T(8,128)S(1)}, f32[6,2,128,128]{3,2,1,0:T(8,128)}, u32[]{:S(2)}) %copy-start.2) | copy-done | bytes 786456
  4.3 0.0 copy-start.3
  4.3 0.9 %copy-done.3 = f32[2,128,128]{2,1,0:T(8,128)S(1)} copy-done((f32[2,128,128]{2,1,0:T(8,128)S(1)}, f32[2,128,128]{2,1,0:T(8,128)}, u32[]{:S(2)}) %copy-start.3) | copy-done | bytes 131096
  5.2 62.7 %shard_map.59 = (f32[2,6,128,128]{3,2,1,0:T(8,128)S(1)}, f32[16,8]{1,0:T(8,128)S(1)}) custom-call(f32[2,3,2,128,128]{4,3,2,1,0:T(8,128)S(1)} %copy-done.1, f32[16,6,32,128]{3,2,1,0:T(8,128)S(1)} %bitcast.2, f32[2,128,128]{2,1,0:T(8,128)S(1)} %copy-done.3, f32[6,2,128,128]{3,2,1,0:T(8,128)S(1)} %copy-done.2), custom_call_target="tpu_custom_call" | custom-call | tf_op jit(solution)/shard_map/pallas_call | solution.py:443
  68.0 0.7 copy.6
  68.6 0.9 %copy.8 = f32[2,3,2,128,128]{4,3,2,1,0:T(8,128)} copy(f32[2,3,2,128,128]{4,3,2,1,0:T(8,128)S(1)} %bitcast.3) | data formatting | bytes 1572864
Async XLA Ops:
  0.6 1.4 %copy-start = (f32[16,3,2,32,128]{4,3,2,1,0:T(8,128)S(1)}, f32[16,3,2,32,128]{4,3,2,1,0:T(8,128)}, u32[]{:S(2)}) copy-start(f32[16,3,2,32,128]{4,3,2,1,0:T(8,128)} %param.5) | copy-start | bytes 4718596
  2.0 1.1 %copy-start.1 = (f32[2,3,2,128,128]{4,3,2,1,0:T(8,128)S(1)}, f32[2,3,2,128,128]{4,3,2,1,0:T(8,128)}, u32[]{:S(2)}) copy-start(f32[2,3,2,128,128]{4,3,2,1,0:T(8,128)} %probes_ref.1) | copy-start | bytes 2359300
  3.2 1.1 %copy-start.2 = (f32[6,2,128,128]{3,2,1,0:T(8,128)S(1)}, f32[6,2,128,128]{3,2,1,0:T(8,128)}, u32[]{:S(2)}) copy-start(f32[6,2,128,128]{3,2,1,0:T(8,128)} %tangent_ref.1) | copy-start | bytes 2359300
  4.3 0.9 %copy-start.3 = (f32[2,128,128]{2,1,0:T(8,128)S(1)}, f32[2,128,128]{2,1,0:T(8,128)}, u32[]{:S(2)}) copy-start(f32[2,128,128]{2,1,0:T(8,128)} %modulus_ref.1) | copy-start | bytes 393220

commit v2 on v1

--- a/solution.py
+++ b/solution.py
@@ -111,16 +111,16 @@
             device_id_type=MESH,
         )
 
-    def halo_copy(stage, r, way):
+    def halo_copy(stage, r, c, way):
         if stage == 0:
-            source, into = probes_ref.at[r, :, (0, depth - 1)[way]], v0
+            source, into = probes_ref.at[r, c, (0, depth - 1)[way]], v0
         else:
-            source, into = v1.at[r, :, (1, depth)[way], pl.ds(PAD, height), :], v1
+            source, into = v1.at[r, c, (1, depth)[way], pl.ds(PAD, height), :], v1
         return pltpu.make_async_remote_copy(
             src_ref=source,
-            dst_ref=into.at[r, :, lands[way], pl.ds(PAD, height), :],
-            send_sem=halo_send.at[stage, r, way],
-            recv_sem=halo_recv.at[stage, r, way],
+            dst_ref=into.at[r, c, lands[way], pl.ds(PAD, height), :],
+            send_sem=halo_send.at[stage, r, c, way],
+            recv_sem=halo_recv.at[stage, r, c, way],
             device_id={"slab": towards[way]},
             device_id_type=MESH,
         )
@@ -130,12 +130,16 @@
         def _():
             act()
 
-    for way in range(2):
-        def begin(way=way):
-            mod_copy(way).start()
-            for r in range(mine):
-                halo_copy(0, r, way).start()
-        guarded(can_send[way], begin)
+    def send_probe(r):
+        for way in range(2):
+            def begin(way=way):
+                if r == 0:
+                    mod_copy(way).start()
+                for c in range(3):
+                    halo_copy(0, r, c, way).start()
+            guarded(can_send[way], begin)
+
+    send_probe(0)
 
     def products(first, second, acc_ref, rows_at, cols_at, mirror_at):
         def step(f, accs):
@@ -222,46 +226,57 @@
 
     lax.fori_loop(0, depth, coefficients, 0)
 
-    def halo_products(stage, r, way):
+    def apply(stage, r, c):
         v, g = ((v0, g0), (v1, g1))[stage]
-        plane = lands[way]
-        for c in range(3):
-            g[r, c, plane] = mod[plane] * v[r, c, plane]
-
-    def apply(stage, r):
-        v, g = ((v0, g0), (v1, g1))[stage]
+        others = [k for k in range(3) if k != c]
+        couple = [3 + c + k - 1 for k in others]
 
         def body(z, carry):
             for start in range(0, height, rows):
                 here = pl.ds(start, rows)
                 inner = pl.ds(PAD + start, rows)
                 m = mod[z + 1, inner, :]
-                vec = [v[r, c, z + 1, inner, :] for c in range(3)]
-                cross = [0.125 * ten[3 + c, z, here, :] for c in range(3)]
-                mixed = (
-                    cross[0] * vec[1] + cross[1] * vec[2],
-                    cross[0] * vec[0] + cross[2] * vec[2],
-                    cross[1] * vec[0] + cross[2] * vec[1],
+                out = diag[c, z, here, :] * v[r, c, z + 1, inner, :]
+                for k, e in zip(others, couple):
+                    out = out + (0.125 * ten[e, z, here, :]) * v[r, k, z + 1, inner, :]
+                near = m * neighbour_sum(v, (r, c), z + 1, start, rows) + neighbour_sum(
+                    g, (r, c), z + 1, start, rows
                 )
-                for c in range(3):
-                    out = diag[c, z, here, :] * vec[c] + mixed[c]
-                    near = m * neighbour_sum(v, (r, c), z + 1, start, rows) + neighbour_sum(
-                        g, (r, c), z + 1, start, rows
-                    )
-                    out = out - 0.0625 * near
-                    if stage == 0:
-                        v1[r, c, z + 1, inner, :] = out
-                        g1[r, c, z + 1, inner, :] = m * out
-                    else:
-                        filt[r, c * depth + z, here, :] = 2.0 * out - v0[r, c, z + 1, inner, :]
+                out = out - 0.0625 * near
+                if stage == 0:
+                    v1[r, c, z + 1, inner, :] = out
+                    g1[r, c, z + 1, inner, :] = m * out
+                else:
+                    filt[r, c * depth + z, here, :] = 2.0 * out - v0[r, c, z + 1, inner, :]
             return carry
 
         lax.fori_loop(0, depth, body, 0)
 
-    def wait_halo(stage, r):
+    def wait_halo(stage, r, c):
+        v, g = ((v0, g0), (v1, g1))[stage]
         for way in range(2):
-            guarded(can_recv[way], lambda way=way: halo_copy(stage, r, way).wait_recv())
-            halo_products(stage, r, way)
+            guarded(can_recv[way], lambda way=way: halo_copy(stage, r, c, way).wait_recv())
+            plane = lands[way]
+            g[r, c, plane] = mod[plane] * v[r, c, plane]
+
+    order = sorted(range(1, groups), key=lambda o: (abs(o - groups // 2), o))
+
+    def there_copy(r, c, o):
+        to = lax.rem(group + o, groups)
+        part = pl.ds(c * depth, depth)
+        return pltpu.make_async_remote_copy(
+            src_ref=filt.at[r, part, pl.ds(pl.multiple_of(to * share, share), share), :],
+            dst_ref=every.at[group * mine + r, part],
+            send_sem=there_send.at[r, c, o],
+            recv_sem=there_recv.at[r, c, o],
+            device_id={"probe": to},
+            device_id_type=MESH,
+        )
+
+    own_rows = pl.ds(pl.multiple_of(group * share, share), share)
+
+    def keep_copy(r):
+        return pltpu.make_async_copy(filt.at[r, :, own_rows, :], every.at[group * mine + r], own_sem.at[r])
 
     for r in range(mine):
         loads[3 + r].wait()
@@ -271,35 +286,22 @@
                 blank = jnp.zeros((PAD, LANES), jnp.float32)
                 g1[r, c, z, pl.ds(0, PAD), :] = blank
                 g1[r, c, z, pl.ds(PAD + height, PAD), :] = blank
-        wait_halo(0, r)
-        apply(0, r)
-        for way in range(2):
-            guarded(can_send[way], lambda way=way, r=r: halo_copy(1, r, way).start())
-
-    partial = share_finish(slots_q, "slab", slab, slabs, sum_send.at[0], sum_recv.at[0])
-    share_start(slots_qp, "probe", group, groups, sump_send.at[0], sump_recv.at[0], partial)
-
-    order = sorted(range(1, groups), key=lambda o: (abs(o - groups // 2), o))
-
-    def there_copy(r, o):
-        to = lax.rem(group + o, groups)
-        return pltpu.make_async_remote_copy(
-            src_ref=filt.at[r, :, pl.ds(pl.multiple_of(to * share, share), share), :],
-            dst_ref=every.at[group * mine + r],
-            send_sem=there_send.at[r, o],
-            recv_sem=there_recv.at[r, o],
-            device_id={"probe": to},
-            device_id_type=MESH,
-        )
-
-    own_rows = pl.ds(pl.multiple_of(group * share, share), share)
-    for r in range(mine):
-        wait_halo(1, r)
-        apply(1, r)
-        for o in order:
-            there_copy(r, o).start()
-        keep = pltpu.make_async_copy(filt.at[r, :, own_rows, :], every.at[group * mine + r], own_sem.at[r])
-        keep.start()
+        for c in range(3):
+            wait_halo(0, r, c)
+            apply(0, r, c)
+            for way in range(2):
+                guarded(can_send[way], lambda way=way, r=r, c=c: halo_copy(1, r, c, way).start())
+        if r + 1 < mine:
+            send_probe(r + 1)
+        if r == 0:
+            partial = share_finish(slots_q, "slab", slab, slabs, sum_send.at[0], sum_recv.at[0])
+            share_start(slots_qp, "probe", group, groups, sump_send.at[0], sump_recv.at[0], partial)
+        for c in range(3):
+            wait_halo(1, r, c)
+            apply(1, r, c)
+            for o in order:
+                there_copy(r, c, o).start()
+        keep_copy(r).start()
 
     gram_q = share_finish(slots_qp, "probe", group, groups, sump_send.at[0], sump_recv.at[0])
     square = (known, LANES)
@@ -320,9 +322,10 @@
         return [ids[i : i + GROUP] for i in range(0, groups, GROUP)]
 
     for r in range(mine):
-        pltpu.make_async_copy(filt.at[r, :, own_rows, :], every.at[group * mine + r], own_sem.at[r]).wait()
-        for o in order:
-            there_copy(r, o).wait_recv()
+        keep_copy(r).wait()
+        for c in range(3):
+            for o in order:
+                there_copy(r, c, o).wait_recv()
         for ids in batch(r):
             for i in range(0, known, GROUP):
                 left = list(range(i, i + GROUP))
@@ -409,22 +412,21 @@
         make(group * mine + r)
         own_copy(r).start()
 
-    corr = lax.dot_general(
-        inverse[...], cross, nt, precision=lax.Precision.HIGHEST, preferred_element_type=jnp.float32
-    )
-    corr_ref[...] = corr * scale
+    corr_ref[...] = coeff[:, :known] * scale
 
     for way in range(2):
         def finish(way=way):
             mod_copy(way).wait_send()
             for stage in range(2):
                 for r in range(mine):
-                    halo_copy(stage, r, way).wait_send()
+                    for c in range(3):
+                        halo_copy(stage, r, c, way).wait_send()
         guarded(can_send[way], finish)
     for r in range(mine):
         own_copy(r).wait()
         for o in order:
-            there_copy(r, o).wait_send()
+            for c in range(3):
+                there_copy(r, c, o).wait_send()
             back_copy(r, o).wait()
 
 
@@ -439,12 +441,12 @@
     f32 = jnp.float32
     padded = (mine, parts, depth + 2, height + 2 * PAD, width)
     dma = pltpu.SemaphoreType.DMA
-    anywhere = pl.BlockSpec(memory_space=pl.ANY)
+    anywhere = pl.BlockSpec(memory_space=pltpu.HBM)
     basis, corr = pl.pallas_call(
         functools.partial(kernel, slabs, groups, scale),
         out_shape=(
             jax.ShapeDtypeStruct((mine, fields, height, width), f32),
-            jax.ShapeDtypeStruct((known, total), f32),
+            jax.ShapeDtypeStruct((total, known), f32),
         ),
         in_specs=[anywhere] * 4,
         out_specs=(anywhere, pl.BlockSpec(memory_space=pltpu.VMEM)),
@@ -469,12 +471,12 @@
             pltpu.VMEM((known, LANES), f32),
             pltpu.VMEM((total, LANES), f32),
             dma((3 + mine,)),
-            dma((2, mine, 2)),
-            dma((2, mine, 2)),
+            dma((2, mine, parts, 2)),
+            dma((2, mine, parts, 2)),
             dma((2,)),
             dma((2,)),
-            dma((mine, groups)),
-            dma((mine, groups)),
+            dma((mine, parts, groups)),
+            dma((mine, parts, groups)),
             dma((mine, groups)),
             dma((mine, groups)),
             dma((2, slabs)),
@@ -484,10 +486,10 @@
             dma((2 * mine,)),
         ],
         compiler_params=pltpu.CompilerParams(
-            collective_id=0, has_side_effects=True, vmem_limit_bytes=40 * 1024 * 1024
+            collective_id=0, has_side_effects=True, vmem_limit_bytes=60 * 1024 * 1024
         ),
     )(probes, earlier.reshape(known, fields, share, width), modulus, tangent)
-    return basis.reshape(probes.shape), corr
+    return basis.reshape(probes.shape), corr.T
 
 
 def solution(mesh):

time: 70.3 us -> 63.7 us (0.906)
  local copies, waits for them, and re-layouts: 6.11 us -> 2.66 us
  Pallas kernels: 62.7 us -> 59.7 us
    unnamed x10 -> x4, local copies, waits for them, and re-layouts: 6.11 us -> 2.66 us
    pallas_call x1, Pallas kernels: 62.7 us -> 59.7 us  [body(): pl.pallas_call(functools.partial(kernel, slabs, groups, scale), out_shape...]
where the time goes in v2:
time: 63.7 us; the launch traced here: 63 us
  Pallas kernels  59.7 us (94%)
  local copies, waits for them, and re-layouts  2.66 us (4%)
  between operations  0.65 us (1%)
    pallas_call x1, Pallas kernels, body(): pl.pallas_call(functools.partial(kernel, slabs, groups, scale), out_shape...  59.7 us
    unnamed x4, local copies, waits for them, and re-layouts  2.66 us

profile of v2, /device:TPU:0, one launch (start us, length us, event | category | flops | bytes accessed | tf_op | source)
XLA Modules:
  0.0 63.0 jit_solution(17898601666804677704)
XLA Ops:
  0.6 59.7 %shard_map.59 = (f32[2,6,128,128]{3,2,1,0:T(8,128)}, f32[8,16]{1,0:T(8,128)}) custom-call(f32[2,3,2,128,128]{4,3,2,1,0:T(8,128)} %probes_ref.1, f32[16,6,32,128]{3,2,1,0:T(8,128)} %bitcast.3, f32[2,128,128]{2,1,0:T(8,128)} %modulus_ref.1, f32[6,2,128,128]{3,2,1,0:T(8,128)} %tangent_ref.1), custom_call_target="tpu_custom_call" | custom-call | tf_op jit(solution)/shard_map/pallas_call | solution.py:445
  60.3 0.0 copy-start
  60.3 2.1 %copy.8 = f32[2,3,2,128,128]{4,3,2,1,0:T(8,128)} copy(f32[2,3,2,128,128]{4,3,2,1,0:T(8,128)} %bitcast.4) | data formatting | bytes 1572864
  62.4 0.0 copy-done
  62.4 0.6 copy.9
Async XLA Ops:
  60.3 2.1 %copy-start = (f32[8,16]{1,0:T(8,128)S(1)}, f32[8,16]{1,0:T(8,128)}, u32[]{:S(2)}) copy-start(f32[8,16]{1,0:T(8,128)} %get-tuple-element.5) | copy-start | bytes 1540

commit v3 on v2

--- a/solution.py
+++ b/solution.py
@@ -35,7 +35,7 @@
 
 
 def kernel(
-    slabs, groups, scale,
+    slabs, groups,
     probes_ref, earlier_ref, modulus_ref, tangent_ref,
     basis_ref, corr_ref,
     v0, v1, g0, g1, mod, ten, diag, quick, filt, every, outgoing,
@@ -64,8 +64,8 @@
                 load_sem.at[3 + r],
             )
         )
-    for copy in loads:
-        copy.start()
+    for i in [0] + list(range(3, 3 + mine)) + [1, 2]:
+        loads[i].start()
 
     barrier = pltpu.get_barrier_semaphore()
     for o in range(1, slabs):
@@ -141,7 +141,7 @@
 
     send_probe(0)
 
-    def products(first, second, acc_ref, rows_at, cols_at, mirror_at):
+    def products(first, second, acc_ref, rows_at, cols_at, mirror_at, begin, end, fresh):
         def step(f, accs):
             left = [ref[k, f] for ref, k in first]
             right = [ref[k, f] for ref, k in second]
@@ -158,7 +158,11 @@
             return tuple(out)
 
         zero = jnp.zeros((8, LANES), jnp.float32)
-        accs = lax.fori_loop(0, fields, step, (zero,) * (len(first) * len(second)))
+        if fresh:
+            accs = (zero,) * (len(first) * len(second))
+        else:
+            accs = tuple(acc_ref[col, row] for col in cols_at for row in rows_at)
+        accs = lax.fori_loop(begin, end, step, accs)
         n = 0
         for i in range(len(first)):
             for j in range(len(second)):
@@ -198,17 +202,6 @@
         for i in range(1, count):
             value = value + slots[i]
         return value
-
-    loads[2].wait()
-    for i in range(0, known, GROUP):
-        for j in range(i, known, GROUP):
-            left = list(range(i, i + GROUP))
-            right = list(range(j, j + GROUP))
-            products(
-                [(quick, k) for k in left], [(quick, k) for k in right], acc_q, right, left,
-                (lambda a, b, left=left, right=right: (right[b], left[a])) if i != j else None,
-            )
-    share_start(slots_q, "slab", slab, slabs, sum_send.at[0], sum_recv.at[0], collapse(acc_q, known, known))
 
     loads[0].wait()
     loads[1].wait()
@@ -294,6 +287,18 @@
         if r + 1 < mine:
             send_probe(r + 1)
         if r == 0:
+            loads[2].wait()
+            for i in range(0, known, GROUP):
+                for j in range(i, known, GROUP):
+                    left = list(range(i, i + GROUP))
+                    right = list(range(j, j + GROUP))
+                    products(
+                        [(quick, k) for k in left], [(quick, k) for k in right], acc_q, right, left,
+                        (lambda a, b, left=left, right=right: (right[b], left[a])) if i != j else None,
+                        0, fields, True,
+                    )
+            share_start(slots_q, "slab", slab, slabs, sum_send.at[0], sum_recv.at[0], collapse(acc_q, known, known))
+        if r == mine - 1:
             partial = share_finish(slots_q, "slab", slab, slabs, sum_send.at[0], sum_recv.at[0])
             share_start(slots_qp, "probe", group, groups, sump_send.at[0], sump_recv.at[0], partial)
         for c in range(3):
@@ -326,20 +331,22 @@
         for c in range(3):
             for o in order:
                 there_copy(r, c, o).wait_recv()
-        for ids in batch(r):
-            for i in range(0, known, GROUP):
-                left = list(range(i, i + GROUP))
-                products([(quick, k) for k in left], [(every, k) for k in ids], acc_y, ids, left, None)
-            for before in range(r + 1):
-                for old in batch(before):
-                    if before == r and old[0] > ids[0]:
-                        continue
-                    same = old == ids
-                    products(
-                        [(every, k) for k in old], [(every, k) for k in ids], acc_y, ids,
-                        [known + k for k in old],
-                        None if same else (lambda a, b, old=old, ids=ids: (known + ids[b], old[a])),
-                    )
+            span = (c * depth, (c + 1) * depth, c == 0)
+            for ids in batch(r):
+                for i in range(0, known, GROUP):
+                    left = list(range(i, i + GROUP))
+                    products([(quick, k) for k in left], [(every, k) for k in ids], acc_y, ids, left, None, *span)
+                for before in range(r + 1):
+                    for old in batch(before):
+                        if before == r and old[0] > ids[0]:
+                            continue
+                        same = old == ids
+                        products(
+                            [(every, k) for k in old], [(every, k) for k in ids], acc_y, ids,
+                            [known + k for k in old],
+                            None if same else (lambda a, b, old=old, ids=ids: (known + ids[b], old[a])),
+                            *span,
+                        )
     part = collapse(acc_y, known + total, total)
     share_start(slots_y, "slab", slab, slabs, sum_send.at[1], sum_recv.at[1], part)
     part = share_finish(slots_y, "slab", slab, slabs, sum_send.at[1], sum_recv.at[1])
@@ -369,7 +376,7 @@
         lead = spread(work[k : k + 1, :], flat) / pivot
         factor = jnp.where(line == k, pivot, factor)
         work = jnp.where(line > k, work - column * lead, work)
-    mixing[...] = work * (scale / jnp.sqrt(factor))
+    mixing[...] = work / jnp.sqrt(factor)
 
     def make(i):
         weights = mixing[pl.ds(i, 1), :]
@@ -412,7 +419,7 @@
         make(group * mine + r)
         own_copy(r).start()
 
-    corr_ref[...] = coeff[:, :known] * scale
+    corr_ref[...] = coeff[:, :known]
 
     for way in range(2):
         def finish(way=way):
@@ -443,7 +450,7 @@
     dma = pltpu.SemaphoreType.DMA
     anywhere = pl.BlockSpec(memory_space=pltpu.HBM)
     basis, corr = pl.pallas_call(
-        functools.partial(kernel, slabs, groups, scale),
+        functools.partial(kernel, slabs, groups),
         out_shape=(
             jax.ShapeDtypeStruct((mine, fields, height, width), f32),
             jax.ShapeDtypeStruct((total, known), f32),
@@ -489,7 +496,7 @@
             collective_id=0, has_side_effects=True, vmem_limit_bytes=60 * 1024 * 1024
         ),
     )(probes, earlier.reshape(known, fields, share, width), modulus, tangent)
-    return basis.reshape(probes.shape), corr.T
+    return basis.reshape(probes.shape) * scale, corr.T * scale
 
 
 def solution(mesh):

time: 63.7 us -> 63.2 us (level)
  other arithmetic: 0 us -> 2.68 us
  local copies, waits for them, and re-layouts: 2.66 us -> 0.01 us
    mul x0 -> x2, other arithmetic: none -> 2.68 us  [body(): return (basis.reshape(probes.shape) * scale, corr.T * scale)]
    unnamed x4 -> x2, local copies, waits for them, and re-layouts: 2.66 us -> 0.01 us
where the time goes in v3:
time: 63.2 us; the launch traced here: 62.5 us
  Pallas kernels  59.1 us (94%)
  other arithmetic  2.68 us (4%)
  between operations  0.65 us (1%)
    pallas_call x1, Pallas kernels, body(): pl.pallas_call(functools.partial(kernel, slabs, groups), out_shape=(jax.S...  59.1 us
    mul x2, other arithmetic, body(): return (basis.reshape(probes.shape) * scale, corr.T * scale)  2.68 us

profile of v3, /device:TPU:0, one launch (start us, length us, event | category | flops | bytes accessed | tf_op | source)
XLA Modules:
  0.0 62.5 jit_solution(14932609648105860436)
XLA Ops:
  0.6 59.1 %shard_map.59 = (f32[2,6,128,128]{3,2,1,0:T(8,128)}, f32[8,16]{1,0:T(8,128)}) custom-call(f32[2,3,2,128,128]{4,3,2,1,0:T(8,128)} %probes_ref.1, f32[16,6,32,128]{3,2,1,0:T(8,128)} %bitcast.4, f32[2,128,128]{2,1,0:T(8,128)} %modulus_ref.1, f32[6,2,128,128]{3,2,1,0:T(8,128)} %tangent_ref.1), custom_call_target="tpu_custom_call" | custom-call | tf_op jit(solution)/shard_map/pallas_call | solution.py:452
  59.8 0.0 copy-start
  59.8 2.1 %broadcast_multiply_fusion = f32[2,6,128,128]{3,2,1,0:T(8,128)} fusion(f32[2,6,128,128]{3,2,1,0:T(8,128)} %get-tuple-element.4), kind=kLoop, calls=%fused_computation | loop fusion | flops 196608 | bytes 1572864 | tf_op jit(solution)/shard_map/mul | solution.py:499
  61.9 0.0 copy-done
  61.9 0.6 multiply_bitcast_fusion
Async XLA Ops:
  59.8 2.1 %copy-start = (f32[8,16]{1,0:T(8,128)S(1)}, f32[8,16]{1,0:T(8,128)}, u32[]{:S(2)}) copy-start(f32[8,16]{1,0:T(8,128)} %get-tuple-element.5) | copy-start | bytes 1540

commit v4 on v3

--- a/solution.py
+++ b/solution.py
@@ -11,6 +11,7 @@
 LANES = 128
 PAD = 8
 GROUP = 4
+EDGE = 2
 
 
 def neighbour_sum(ref, lead, z, start, rows):
@@ -38,11 +39,12 @@
     slabs, groups,
     probes_ref, earlier_ref, modulus_ref, tangent_ref,
     basis_ref, corr_ref,
-    v0, v1, g0, g1, mod, ten, diag, quick, filt, every, outgoing,
+    v0, v1, g0, g1, t0, t1, h0, h1, mod, ten, diag, tmod, tten, tdiag, quick, filt, every, outgoing,
     acc_q, acc_y, slots_q, slots_qp, slots_y, slots_yp, inverse, mixing,
     load_sem, halo_send, halo_recv, mod_send, mod_recv,
     there_send, there_recv, back_send, back_recv,
     sum_send, sum_recv, sump_send, sump_recv, own_sem,
+    raw_send, raw_recv, raw_own, quarter_send, quarter_recv,
 ):
     slab = lax.axis_index("slab")
     group = lax.axis_index("probe")
@@ -50,13 +52,15 @@
     known, fields, share, _ = earlier_ref.shape
     total = mine * groups
     rows = 32
+    first = mine - 1
+    wide = share + 2 * PAD
 
     loads = [
         pltpu.make_async_copy(modulus_ref, mod.at[pl.ds(1, depth), pl.ds(PAD, height), :], load_sem.at[0]),
-        pltpu.make_async_copy(tangent_ref, ten, load_sem.at[1]),
+        pltpu.make_async_copy(tangent_ref, ten.at[:, :, pl.ds(PAD, height), :], load_sem.at[1]),
         pltpu.make_async_copy(earlier_ref, quick, load_sem.at[2]),
     ]
-    for r in range(mine):
+    for r in range(first):
         loads.append(
             pltpu.make_async_copy(
                 probes_ref.at[r],
@@ -64,7 +68,7 @@
                 load_sem.at[3 + r],
             )
         )
-    for i in [0] + list(range(3, 3 + mine)) + [1, 2]:
+    for i in [0] + list(range(3, 3 + first)) + [1, 2]:
         loads[i].start()
 
     barrier = pltpu.get_barrier_semaphore()
@@ -77,14 +81,37 @@
         edge = jnp.zeros(ref.shape[:3] + (PAD, LANES), jnp.float32)
         ref[:, :, :, pl.ds(0, PAD), :] = edge
         ref[:, :, :, pl.ds(PAD + height, PAD), :] = edge
+    for ref in (ten, diag):
+        edge = jnp.zeros(ref.shape[:2] + (PAD, LANES), jnp.float32)
+        ref[:, :, pl.ds(0, PAD), :] = edge
+        ref[:, :, pl.ds(PAD + height, PAD), :] = edge
+    for ref in (t0, t1):
+        edge = jnp.zeros(ref.shape[:3] + (PAD - EDGE, LANES), jnp.float32)
+        ref[:, :, :, pl.ds(0, PAD - EDGE), :] = edge
+        ref[:, :, :, pl.ds(PAD + share + EDGE, PAD - EDGE), :] = edge
     edge = jnp.zeros((depth + 2, PAD, LANES), jnp.float32)
     mod[:, pl.ds(0, PAD), :] = edge
     mod[:, pl.ds(PAD + height, PAD), :] = edge
 
     def clear(plane):
         for ref in (v0, v1):
-            ref[:, :, plane, pl.ds(PAD, height), :] = jnp.zeros((mine, 3, height, LANES), jnp.float32)
+            ref[:, :, plane, pl.ds(PAD, height), :] = jnp.zeros((first, 3, height, LANES), jnp.float32)
+        for ref in (t0, t1):
+            ref[:, :, plane] = jnp.zeros((groups, 3, wide, LANES), jnp.float32)
         mod[plane, pl.ds(PAD, height), :] = jnp.zeros((height, LANES), jnp.float32)
+
+    def clear_rows(ref, start):
+        count = ref.shape[0]
+        blank = jnp.zeros((count, 3, depth, EDGE, LANES), jnp.float32)
+        ref[:, :, pl.ds(1, depth), pl.ds(start, EDGE), :] = blank
+
+    @pl.when(group == 0)
+    def _():
+        clear_rows(t0, PAD - EDGE)
+
+    @pl.when(group == groups - 1)
+    def _():
+        clear_rows(t0, PAD + share)
 
     @pl.when(slab == 0)
     def _():
@@ -139,7 +166,73 @@
                     halo_copy(0, r, c, way).start()
             guarded(can_send[way], begin)
 
+    def raw_part(kind, to):
+        return (
+            pl.ds(pl.multiple_of(to * share, share), share),
+            pl.ds(to * share - EDGE, EDGE),
+            pl.ds(to * share + share, EDGE),
+        )[kind]
+
+    raw_rows = (pl.ds(PAD, share), pl.ds(PAD - EDGE, EDGE), pl.ds(PAD + share, EDGE))
+
+    def raw_copy(kind, o, arriving=False):
+        to = lax.rem(group + o, groups)
+        landing = t0.at[group, :, pl.ds(1, depth), raw_rows[kind], :]
+        return pltpu.make_async_remote_copy(
+            src_ref=landing if arriving else probes_ref.at[first, :, :, raw_part(kind, to), :],
+            dst_ref=t0.at[group, :, pl.ds(1, depth), raw_rows[kind], :],
+            send_sem=raw_send.at[kind, o],
+            recv_sem=raw_recv.at[kind, o],
+            device_id={"probe": to},
+            device_id_type=MESH,
+        )
+
+    def raw_local(kind):
+        return pltpu.make_async_copy(
+            probes_ref.at[first, :, :, raw_part(kind, group), :],
+            t0.at[group, :, pl.ds(1, depth), raw_rows[kind], :],
+            raw_own.at[kind],
+        )
+
+    def in_mesh(kind, to):
+        return (None, to > 0, to < groups - 1)[kind]
+
+    def maybe(condition, act):
+        if condition is None:
+            act()
+        else:
+            guarded(condition, act)
+
+    order = sorted(range(1, groups), key=lambda o: (abs(o - groups // 2), o))
+
     send_probe(0)
+    for kind in range(3):
+        maybe(in_mesh(kind, group), lambda kind=kind: raw_local(kind).start())
+    for o in order:
+        to = lax.rem(group + o, groups)
+        for kind in range(3):
+            maybe(in_mesh(kind, to), lambda kind=kind, o=o: raw_copy(kind, o).start())
+
+    def quarter_copy(stage, o, way):
+        ref = (t0, t1)[stage]
+        source = lax.rem(group + groups - o, groups)
+        span = pl.ds(PAD - EDGE, share + 2 * EDGE)
+        return pltpu.make_async_remote_copy(
+            src_ref=ref.at[source, :, (1, depth)[way], span, :],
+            dst_ref=ref.at[source, :, lands[way], span, :],
+            send_sem=quarter_send.at[stage, o, way],
+            recv_sem=quarter_recv.at[stage, o, way],
+            device_id={"slab": towards[way]},
+            device_id_type=MESH,
+        )
+
+    def quarter_send_all(stage, o):
+        for way in range(2):
+            guarded(can_send[way], lambda way=way: quarter_copy(stage, o, way).start())
+
+    def quarter_wait(stage, o):
+        for way in range(2):
+            guarded(can_recv[way], lambda way=way: quarter_copy(stage, o, way).wait_recv())
 
     def products(first, second, acc_ref, rows_at, cols_at, mirror_at, begin, end, fresh):
         def step(f, accs):
@@ -210,8 +303,8 @@
 
     def coefficients(z, carry):
         for start in range(0, height, rows):
-            here = pl.ds(start, rows)
-            m = mod[z + 1, pl.ds(PAD + start, rows), :]
+            here = pl.ds(PAD + start, rows)
+            m = mod[z + 1, here, :]
             base = (3.4 * m + neighbour_sum(mod, (), z + 1, start, rows)) * 0.0625 - 1.0
             for c in range(3):
                 diag[c, z, here, :] = base + 0.125 * ten[c, z, here, :]
@@ -219,31 +312,56 @@
 
     lax.fori_loop(0, depth, coefficients, 0)
 
-    def apply(stage, r, c):
-        v, g = ((v0, g0), (v1, g1))[stage]
+    def apply(v, g, fields_of, lead, c, chunks, store):
+        mods, diags, tens = fields_of
         others = [k for k in range(3) if k != c]
         couple = [3 + c + k - 1 for k in others]
 
         def body(z, carry):
-            for start in range(0, height, rows):
-                here = pl.ds(start, rows)
-                inner = pl.ds(PAD + start, rows)
-                m = mod[z + 1, inner, :]
-                out = diag[c, z, here, :] * v[r, c, z + 1, inner, :]
+            for start, size in chunks:
+                inner = pl.ds(PAD + start, size)
+                m = mods[z + 1, inner, :]
+                out = diags[c, z, inner, :] * v[lead, c, z + 1, inner, :]
                 for k, e in zip(others, couple):
-                    out = out + (0.125 * ten[e, z, here, :]) * v[r, k, z + 1, inner, :]
-                near = m * neighbour_sum(v, (r, c), z + 1, start, rows) + neighbour_sum(
-                    g, (r, c), z + 1, start, rows
+                    out = out + (0.125 * tens[e, z, inner, :]) * v[lead, k, z + 1, inner, :]
+                near = m * neighbour_sum(v, (lead, c), z + 1, start, size) + neighbour_sum(
+                    g, (lead, c), z + 1, start, size
                 )
-                out = out - 0.0625 * near
-                if stage == 0:
-                    v1[r, c, z + 1, inner, :] = out
-                    g1[r, c, z + 1, inner, :] = m * out
-                else:
-                    filt[r, c * depth + z, here, :] = 2.0 * out - v0[r, c, z + 1, inner, :]
+                store(z, start, size, m, out - 0.0625 * near)
             return carry
 
         lax.fori_loop(0, depth, body, 0)
+
+    def apply_whole(stage, r, c):
+        def store(z, start, size, m, out):
+            inner = pl.ds(PAD + start, size)
+            if stage == 0:
+                v1[r, c, z + 1, inner, :] = out
+                g1[r, c, z + 1, inner, :] = m * out
+            else:
+                filt[r, c * depth + z, pl.ds(start, size), :] = 2.0 * out - v0[r, c, z + 1, inner, :]
+
+        chunks = [(start, rows) for start in range(0, height, rows)]
+        v, g = ((v0, g0), (v1, g1))[stage]
+        apply(v, g, (mod, diag, ten), r, c, chunks, store)
+
+    def apply_quarter(stage, source, c):
+        def store(z, start, size, m, out):
+            inner = pl.ds(PAD + start, size)
+            if stage == 0:
+                t1[source, c, z + 1, inner, :] = out
+            else:
+                every[source * mine + first, c * depth + z] = 2.0 * out - t0[source, c, z + 1, inner, :]
+
+        chunks = [(-4, share + 8)] if stage == 0 else [(0, share)]
+        v, g = ((t0, h0), (t1, h1))[stage]
+        apply(v, g, (tmod, tdiag, tten), source, c, chunks, store)
+
+    def quarter_products(stage, source):
+        v, g = ((t0, h0), (t1, h1))[stage]
+        for c in range(3):
+            for plane in range(depth + 2):
+                g[source, c, plane] = tmod[plane] * v[source, c, plane]
 
     def wait_halo(stage, r, c):
         v, g = ((v0, g0), (v1, g1))[stage]
@@ -251,8 +369,6 @@
             guarded(can_recv[way], lambda way=way: halo_copy(stage, r, c, way).wait_recv())
             plane = lands[way]
             g[r, c, plane] = mod[plane] * v[r, c, plane]
-
-    order = sorted(range(1, groups), key=lambda o: (abs(o - groups // 2), o))
 
     def there_copy(r, c, o):
         to = lax.rem(group + o, groups)
@@ -271,7 +387,7 @@
     def keep_copy(r):
         return pltpu.make_async_copy(filt.at[r, :, own_rows, :], every.at[group * mine + r], own_sem.at[r])
 
-    for r in range(mine):
+    for r in range(first):
         loads[3 + r].wait()
         for c in range(3):
             for z in range(1, depth + 1):
@@ -281,32 +397,75 @@
                 g1[r, c, z, pl.ds(PAD + height, PAD), :] = blank
         for c in range(3):
             wait_halo(0, r, c)
-            apply(0, r, c)
+            apply_whole(0, r, c)
             for way in range(2):
                 guarded(can_send[way], lambda way=way, r=r, c=c: halo_copy(1, r, c, way).start())
-        if r + 1 < mine:
+        if r + 1 < first:
             send_probe(r + 1)
-        if r == 0:
-            loads[2].wait()
-            for i in range(0, known, GROUP):
-                for j in range(i, known, GROUP):
-                    left = list(range(i, i + GROUP))
-                    right = list(range(j, j + GROUP))
-                    products(
-                        [(quick, k) for k in left], [(quick, k) for k in right], acc_q, right, left,
-                        (lambda a, b, left=left, right=right: (right[b], left[a])) if i != j else None,
-                        0, fields, True,
-                    )
-            share_start(slots_q, "slab", slab, slabs, sum_send.at[0], sum_recv.at[0], collapse(acc_q, known, known))
-        if r == mine - 1:
-            partial = share_finish(slots_q, "slab", slab, slabs, sum_send.at[0], sum_recv.at[0])
-            share_start(slots_qp, "probe", group, groups, sump_send.at[0], sump_recv.at[0], partial)
+
+    take = pl.ds(pl.multiple_of(group * share, share), wide)
+    for plane in range(depth + 2):
+        tmod[plane] = mod[plane, take, :]
+    for z in range(depth):
+        for e in range(6):
+            tten[e, z] = ten[e, z, take, :]
+        for c in range(3):
+            tdiag[c, z] = diag[c, z, take, :]
+
+    for kind in range(3):
+        maybe(in_mesh(kind, group), lambda kind=kind: raw_local(kind).wait())
+    quarter_send_all(0, 0)
+    for o in order:
+        for kind in range(3):
+            maybe(in_mesh(kind, group), lambda kind=kind, o=o: raw_copy(kind, o, True).wait_recv())
+        quarter_send_all(0, o)
+
+    for r in range(first):
         for c in range(3):
             wait_halo(1, r, c)
-            apply(1, r, c)
+            apply_whole(1, r, c)
             for o in order:
                 there_copy(r, c, o).start()
         keep_copy(r).start()
+
+    def source_of(o):
+        return lax.rem(group + groups - o, groups)
+
+    for o in [0] + order:
+        quarter_wait(0, o)
+        quarter_products(0, source_of(o))
+        for c in range(3):
+            apply_quarter(0, source_of(o), c)
+
+        def drop(start, o=o):
+            t1[source_of(o), :, pl.ds(1, depth), pl.ds(start, PAD), :] = jnp.zeros(
+                (3, depth, PAD, LANES), jnp.float32
+            )
+
+        guarded(group == 0, lambda drop=drop: drop(0))
+        guarded(group == groups - 1, lambda drop=drop: drop(PAD + share))
+        quarter_send_all(1, o)
+
+    loads[2].wait()
+    for i in range(0, known, GROUP):
+        for j in range(i, known, GROUP):
+            left = list(range(i, i + GROUP))
+            right = list(range(j, j + GROUP))
+            products(
+                [(quick, k) for k in left], [(quick, k) for k in right], acc_q, right, left,
+                (lambda a, b, left=left, right=right: (right[b], left[a])) if i != j else None,
+                0, fields, True,
+            )
+    share_start(slots_q, "slab", slab, slabs, sum_send.at[0], sum_recv.at[0], collapse(acc_q, known, known))
+
+    for o in [0] + order:
+        quarter_wait(1, o)
+        quarter_products(1, source_of(o))
+        for c in range(3):
+            apply_quarter(1, source_of(o), c)
+
+    partial = share_finish(slots_q, "slab", slab, slabs, sum_send.at[0], sum_recv.at[0])
+    share_start(slots_qp, "probe", group, groups, sump_send.at[0], sump_recv.at[0], partial)
 
     gram_q = share_finish(slots_qp, "probe", group, groups, sump_send.at[0], sump_recv.at[0])
     square = (known, LANES)
@@ -326,17 +485,20 @@
         ids = [p * mine + r for p in range(groups)]
         return [ids[i : i + GROUP] for i in range(0, groups, GROUP)]
 
-    for r in range(mine):
-        keep_copy(r).wait()
-        for c in range(3):
-            for o in order:
-                there_copy(r, c, o).wait_recv()
+    sequence = [first] + list(range(first))
+    for turn, r in enumerate(sequence):
+        if r < first:
+            keep_copy(r).wait()
+        for c in range(3):
+            if r < first:
+                for o in order:
+                    there_copy(r, c, o).wait_recv()
             span = (c * depth, (c + 1) * depth, c == 0)
             for ids in batch(r):
                 for i in range(0, known, GROUP):
                     left = list(range(i, i + GROUP))
                     products([(quick, k) for k in left], [(every, k) for k in ids], acc_y, ids, left, None, *span)
-                for before in range(r + 1):
+                for before in sequence[: turn + 1]:
                     for old in batch(before):
                         if before == r and old[0] > ids[0]:
                             continue
@@ -425,16 +587,23 @@
         def finish(way=way):
             mod_copy(way).wait_send()
             for stage in range(2):
-                for r in range(mine):
+                for r in range(first):
                     for c in range(3):
                         halo_copy(stage, r, c, way).wait_send()
+                for o in range(groups):
+                    quarter_copy(stage, o, way).wait_send()
         guarded(can_send[way], finish)
     for r in range(mine):
         own_copy(r).wait()
         for o in order:
-            for c in range(3):
-                there_copy(r, c, o).wait_send()
+            if r < first:
+                for c in range(3):
+                    there_copy(r, c, o).wait_send()
             back_copy(r, o).wait()
+    for o in order:
+        to = lax.rem(group + o, groups)
+        for kind in range(3):
+            maybe(in_mesh(kind, to), lambda kind=kind, o=o: raw_copy(kind, o).wait_send())
 
 
 def body(probes, earlier, modulus, tangent):
@@ -446,7 +615,8 @@
     fields = parts * depth
     scale = float(parts * depth * slabs * height * width) ** 0.5
     f32 = jnp.float32
-    padded = (mine, parts, depth + 2, height + 2 * PAD, width)
+    padded = (mine - 1, parts, depth + 2, height + 2 * PAD, width)
+    quarter = (groups, parts, depth + 2, share + 2 * PAD, width)
     dma = pltpu.SemaphoreType.DMA
     anywhere = pl.BlockSpec(memory_space=pltpu.HBM)
     basis, corr = pl.pallas_call(
@@ -462,9 +632,16 @@
             pltpu.VMEM(padded, f32),
             pltpu.VMEM(padded, f32),
             pltpu.VMEM(padded, f32),
+            pltpu.VMEM(quarter, f32),
+            pltpu.VMEM(quarter, f32),
+            pltpu.VMEM(quarter, f32),
+            pltpu.VMEM(quarter, f32),
             pltpu.VMEM((depth + 2, height + 2 * PAD, width), f32),
-            pltpu.VMEM((6, depth, height, width), f32),
-            pltpu.VMEM((3, depth, height, width), f32),
+            pltpu.VMEM((6, depth, height + 2 * PAD, width), f32),
+            pltpu.VMEM((3, depth, height + 2 * PAD, width), f32),
+            pltpu.VMEM((depth + 2, share + 2 * PAD, width), f32),
+            pltpu.VMEM((6, depth, share + 2 * PAD, width), f32),
+            pltpu.VMEM((3, depth, share + 2 * PAD, width), f32),
             pltpu.VMEM((known, fields, share, width), f32),
             pltpu.VMEM((mine, fields, height, width), f32),
             pltpu.VMEM((total, fields, share, width), f32),
@@ -491,6 +668,11 @@
             dma((2, groups)),
             dma((2, groups)),
             dma((2 * mine,)),
+            dma((3, groups)),
+            dma((3, groups)),
+            dma((3,)),
+            dma((2, groups, 2)),
+            dma((2, groups, 2)),
         ],
         compiler_params=pltpu.CompilerParams(
             collective_id=0, has_side_effects=True, vmem_limit_bytes=60 * 1024 * 1024

time: 63.2 us -> 65.3 us (1.033)
  Pallas kernels: 59.1 us -> 61.2 us
    pallas_call x1, Pallas kernels: 59.1 us -> 61.2 us  [body(): pl.pallas_call(functools.partial(kernel, slabs, groups), out_shape=(jax.S...]
where the time goes in v4:
time: 65.3 us; the launch traced here: 64.5 us
  Pallas kernels  61.2 us (94%)
  other arithmetic  2.68 us (4%)
    pallas_call x1, Pallas kernels, body(): pl.pallas_call(functools.partial(kernel, slabs, groups), out_shape=(jax.S...  61.2 us
    mul x2, other arithmetic, body(): return (basis.reshape(probes.shape) * scale, corr.T * scale)  2.68 us

profile of v4, /device:TPU:0, one launch (start us, length us, event | category | flops | bytes accessed | tf_op | source)
XLA Modules:
  0.0 64.5 jit_solution(518589977893328090)
XLA Ops:
  0.6 61.2 %shard_map.59 = (f32[2,6,128,128]{3,2,1,0:T(8,128)}, f32[8,16]{1,0:T(8,128)}) custom-call(f32[2,3,2,128,128]{4,3,2,1,0:T(8,128)} %probes_ref.1, f32[16,6,32,128]{3,2,1,0:T(8,128)} %bitcast.4, f32[2,128,128]{2,1,0:T(8,128)} %modulus_ref.1, f32[6,2,128,128]{3,2,1,0:T(8,128)} %tangent_ref.1), custom_call_target="tpu_custom_call" | custom-call | tf_op jit(solution)/shard_map/pallas_call | solution.py:622
  61.8 0.0 copy-start
  61.8 2.1 %broadcast_multiply_fusion = f32[2,6,128,128]{3,2,1,0:T(8,128)} fusion(f32[2,6,128,128]{3,2,1,0:T(8,128)} %get-tuple-element.4), kind=kLoop, calls=%fused_computation | loop fusion | flops 196608 | bytes 1572864 | tf_op jit(solution)/shard_map/mul | solution.py:681
  63.9 0.0 copy-done
  63.9 0.6 multiply_bitcast_fusion
Async XLA Ops:
  61.8 2.1 %copy-start = (f32[8,16]{1,0:T(8,128)S(1)}, f32[8,16]{1,0:T(8,128)}, u32[]{:S(2)}) copy-start(f32[8,16]{1,0:T(8,128)} %get-tuple-element.5) | copy-start | bytes 1540

commit v5 on v4

--- a/solution.py
+++ b/solution.py
@@ -403,48 +403,9 @@
         if r + 1 < first:
             send_probe(r + 1)
 
-    take = pl.ds(pl.multiple_of(group * share, share), wide)
-    for plane in range(depth + 2):
-        tmod[plane] = mod[plane, take, :]
-    for z in range(depth):
-        for e in range(6):
-            tten[e, z] = ten[e, z, take, :]
-        for c in range(3):
-            tdiag[c, z] = diag[c, z, take, :]
-
     for kind in range(3):
         maybe(in_mesh(kind, group), lambda kind=kind: raw_local(kind).wait())
     quarter_send_all(0, 0)
-    for o in order:
-        for kind in range(3):
-            maybe(in_mesh(kind, group), lambda kind=kind, o=o: raw_copy(kind, o, True).wait_recv())
-        quarter_send_all(0, o)
-
-    for r in range(first):
-        for c in range(3):
-            wait_halo(1, r, c)
-            apply_whole(1, r, c)
-            for o in order:
-                there_copy(r, c, o).start()
-        keep_copy(r).start()
-
-    def source_of(o):
-        return lax.rem(group + groups - o, groups)
-
-    for o in [0] + order:
-        quarter_wait(0, o)
-        quarter_products(0, source_of(o))
-        for c in range(3):
-            apply_quarter(0, source_of(o), c)
-
-        def drop(start, o=o):
-            t1[source_of(o), :, pl.ds(1, depth), pl.ds(start, PAD), :] = jnp.zeros(
-                (3, depth, PAD, LANES), jnp.float32
-            )
-
-        guarded(group == 0, lambda drop=drop: drop(0))
-        guarded(group == groups - 1, lambda drop=drop: drop(PAD + share))
-        quarter_send_all(1, o)
 
     loads[2].wait()
     for i in range(0, known, GROUP):
@@ -458,14 +419,49 @@
             )
     share_start(slots_q, "slab", slab, slabs, sum_send.at[0], sum_recv.at[0], collapse(acc_q, known, known))
 
-    for o in [0] + order:
-        quarter_wait(1, o)
-        quarter_products(1, source_of(o))
-        for c in range(3):
-            apply_quarter(1, source_of(o), c)
+    for r in range(first):
+        for c in range(3):
+            wait_halo(1, r, c)
+            apply_whole(1, r, c)
+            for o in order:
+                there_copy(r, c, o).start()
+        keep_copy(r).start()
+
+    for o in order:
+        for kind in range(3):
+            maybe(in_mesh(kind, group), lambda kind=kind, o=o: raw_copy(kind, o, True).wait_recv())
+        quarter_send_all(0, o)
+
 
     partial = share_finish(slots_q, "slab", slab, slabs, sum_send.at[0], sum_recv.at[0])
     share_start(slots_qp, "probe", group, groups, sump_send.at[0], sump_recv.at[0], partial)
+
+    take = pl.ds(pl.multiple_of(group * share, share), wide)
+    for plane in range(depth + 2):
+        tmod[plane] = mod[plane, take, :]
+    for z in range(depth):
+        for e in range(6):
+            tten[e, z] = ten[e, z, take, :]
+        for c in range(3):
+            tdiag[c, z] = diag[c, z, take, :]
+
+    def source_of(o):
+        return lax.rem(group + groups - o, groups)
+
+    for o in [0] + order:
+        quarter_wait(0, o)
+        quarter_products(0, source_of(o))
+        for c in range(3):
+            apply_quarter(0, source_of(o), c)
+
+        def drop(start, o=o):
+            t1[source_of(o), :, pl.ds(1, depth), pl.ds(start, PAD), :] = jnp.zeros(
+                (3, depth, PAD, LANES), jnp.float32
+            )
+
+        guarded(group == 0, lambda drop=drop: drop(0))
+        guarded(group == groups - 1, lambda drop=drop: drop(PAD + share))
+        quarter_send_all(1, o)
 
     gram_q = share_finish(slots_qp, "probe", group, groups, sump_send.at[0], sump_recv.at[0])
     square = (known, LANES)
@@ -481,12 +477,17 @@
     inv = jnp.where(lane < known, inverse[...], 0.0)
     inverse[...] = inv
 
+    def last_stage(o):
+        quarter_wait(1, o)
+        quarter_products(1, source_of(o))
+        for c in range(3):
+            apply_quarter(1, source_of(o), c)
+
     def batch(r):
         ids = [p * mine + r for p in range(groups)]
         return [ids[i : i + GROUP] for i in range(0, groups, GROUP)]
 
-    sequence = [first] + list(range(first))
-    for turn, r in enumerate(sequence):
+    def gather(r):
         if r < first:
             keep_copy(r).wait()
         for c in range(3):
@@ -498,7 +499,7 @@
                 for i in range(0, known, GROUP):
                     left = list(range(i, i + GROUP))
                     products([(quick, k) for k in left], [(every, k) for k in ids], acc_y, ids, left, None, *span)
-                for before in sequence[: turn + 1]:
+                for before in range(r + 1):
                     for old in batch(before):
                         if before == r and old[0] > ids[0]:
                             continue
@@ -509,6 +510,12 @@
                             None if same else (lambda a, b, old=old, ids=ids: (known + ids[b], old[a])),
                             *span,
                         )
+    for o in ([0] + order)[:-1]:
+        last_stage(o)
+    for r in range(first):
+        gather(r)
+    last_stage(order[-1])
+    gather(first)
     part = collapse(acc_y, known + total, total)
     share_start(slots_y, "slab", slab, slabs, sum_send.at[1], sum_recv.at[1], part)
     part = share_finish(slots_y, "slab", slab, slabs, sum_send.at[1], sum_recv.at[1])

time: 65.3 us -> 61.9 us (0.948)
  Pallas kernels: 61.2 us -> 57.7 us
    pallas_call x1, Pallas kernels: 61.2 us -> 57.7 us  [body(): pl.pallas_call(functools.partial(kernel, slabs, groups), out_shape=(jax.S...]
where the time goes in v5:
time: 61.9 us; the launch traced here: 61 us
  Pallas kernels  57.7 us (93%)
  other arithmetic  2.68 us (4%)
  between operations  0.65 us (1%)
    pallas_call x1, Pallas kernels, body(): pl.pallas_call(functools.partial(kernel, slabs, groups), out_shape=(jax.S...  57.7 us
    mul x2, other arithmetic, body(): return (basis.reshape(probes.shape) * scale, corr.T * scale)  2.68 us

profile of v5, /device:TPU:0, one launch (start us, length us, event | category | flops | bytes accessed | tf_op | source)
XLA Modules:
  0.0 61.0 jit_solution(8678311154642745636)
XLA Ops:
  0.6 57.7 %shard_map.59 = (f32[2,6,128,128]{3,2,1,0:T(8,128)}, f32[8,16]{1,0:T(8,128)}) custom-call(f32[2,3,2,128,128]{4,3,2,1,0:T(8,128)} %probes_ref.1, f32[16,6,32,128]{3,2,1,0:T(8,128)} %bitcast.4, f32[2,128,128]{2,1,0:T(8,128)} %modulus_ref.1, f32[6,2,128,128]{3,2,1,0:T(8,128)} %tangent_ref.1), custom_call_target="tpu_custom_call" | custom-call | tf_op jit(solution)/shard_map/pallas_call | solution.py:629
  58.3 0.0 copy-start
  58.3 2.1 %broadcast_multiply_fusion = f32[2,6,128,128]{3,2,1,0:T(8,128)} fusion(f32[2,6,128,128]{3,2,1,0:T(8,128)} %get-tuple-element.4), kind=kLoop, calls=%fused_computation | loop fusion | flops 196608 | bytes 1572864 | tf_op jit(solution)/shard_map/mul | solution.py:688
  60.4 0.0 copy-done
  60.4 0.6 multiply_bitcast_fusion
Async XLA Ops:
  58.3 2.1 %copy-start = (f32[8,16]{1,0:T(8,128)S(1)}, f32[8,16]{1,0:T(8,128)}, u32[]{:S(2)}) copy-start(f32[8,16]{1,0:T(8,128)} %get-tuple-element.5) | copy-start | bytes 1540
